TPU v7x, 32 devices: a whole 2x2x4 slice. The times are simulated.
32 devices in a mesh: ctx: 4 (over y, x), grp: 8 (over z, core).
Axes of the slice: x: 2, y: 2, z: 4, core: 2. Of those that a mesh axis runs over, the one named last changes fastest.
Arguments:
- q_in: bfloat16 [512, 8192], P('ctx', 'grp'), may hold values from -170 to 170
- k_in: bfloat16 [512, 8192], P('ctx', 'grp'), may hold values from -6 to 6
- v_in: bfloat16 [512, 8192], P('ctx', 'grp'), may hold values from -6 to 6
- fir: float32 [3, 3, 8192], P(None, None, 'grp'), may hold values from -3 to 3
- skip: float32 [8192], P('grp'), may hold values from 0.2 to 1
- taps: bfloat16 [64, 512], P('grp'), may hold values from -0.5 to 0.5
- segments: int32 [512], P('ctx'), may hold values from 0 to 1, never falling along the last dimension, each value on 1 to 384 neighbouring positions
- gain: float32 [8192], P('grp'), may hold values from 0.1 to 1.9
Outputs:
- mixed: bfloat16 [512, 8192], P('ctx', 'grp')
All inputs are finite; a program needn't handle non-finite values.
Results may differ from a plain program's by a relative error of at most 0.0085.
Values may be sent and summed in bfloat16 or wider, within the bound.
A program may use at most 64 MiB of HBM per device.

v0:
```python
import jax
import jax.numpy as jnp
from jax import lax
from jax.sharding import PartitionSpec as P

D = 8192
GW = 128


def shifted(value, axis, by):
    peers = lax.axis_size(axis)
    pairs = [(i, i + by) for i in range(peers) if 0 <= i + by < peers]
    return lax.ppermute(value, axis, pairs)


def band_rect(padded_taps, pad_left, lag_base, rows, cols):
    length = rows + cols - 1
    window = lax.dynamic_slice_in_dim(padded_taps, lag_base - cols + 1 + pad_left, length, 0)
    flipped = jnp.concatenate([window[::-1], jnp.zeros((1,), padded_taps.dtype)])
    tiled = jnp.tile(flipped, rows)[: rows * length].reshape(rows, length)
    return tiled[:, rows - 1 :]


def token_conv(product_kv, taps, all_segs, segments):
    rows_dev, width = product_kv.shape
    groups_local = width // GW
    total_rows = all_segs.shape[0]
    my_start = lax.axis_index("ctx") * rows_dev
    margin = jnp.zeros((total_rows,), taps.dtype)
    padded_taps = [jnp.concatenate([margin, taps[group], margin]) for group in range(groups_local)]
    empty = jnp.zeros((rows_dev, width), jnp.float32)
    piece = lax.all_gather(product_kv, "ctx", axis=0, tiled=True)
    count = piece.shape[0]
    needed = (jnp.int32(0) <= my_start + rows_dev - 1) & (all_segs[-1] >= segments[0])
    allowed = segments[:, None] == all_segs[None, :]

    def work(total):
        parts_out = []
        for group in range(groups_local):
            matrix = band_rect(padded_taps[group], total_rows, my_start, rows_dev, count)
            matrix = jnp.where(allowed, matrix, jnp.zeros((), matrix.dtype))
            parts_out.append(
                jnp.dot(
                    matrix,
                    piece[:, group * GW : (group + 1) * GW],
                    preferred_element_type=jnp.float32,
                )
            )
        return total + jnp.concatenate(parts_out, axis=1)

    return lax.cond(needed, work, lambda total: total, empty)


def on_device(q_in, k_in, v_in, fir, skip, taps, segments, gain):
    rows_dev, width = q_in.shape
    stacked = jnp.stack([q_in, k_in, v_in])
    before = shifted(stacked[:, rows_dev - 2 :, :], "ctx", 1)
    padded = jnp.concatenate([before, stacked], axis=1).astype(jnp.float32)
    filtered = (
        fir[:, 0, None, :] * padded[:, 2:]
        + fir[:, 1, None, :] * padded[:, 1:-1]
        + fir[:, 2, None, :] * padded[:, :-2]
    )
    product_kv = (filtered[1] * filtered[2]).astype(jnp.bfloat16)
    all_segs = lax.all_gather(segments, "ctx", axis=0, tiled=True)
    conv = token_conv(product_kv, taps, all_segs, segments)
    gated = filtered[0] * (conv + skip * product_kv.astype(jnp.float32))
    squares = lax.psum(jnp.sum(gated * gated, axis=1), "grp")
    mixed = gated * lax.rsqrt(squares[:, None] / D + 1e-06) * gain
    return mixed.astype(jnp.bfloat16)


def solution(mesh):
    return jax.shard_map(
        on_device,
        mesh=mesh,
        in_specs=(
            P("ctx", "grp"),
            P("ctx", "grp"),
            P("ctx", "grp"),
            P(None, None, "grp"),
            P("grp"),
            P("grp", None),
            P("ctx"),
            P("grp"),
        ),
        out_specs=P("ctx", "grp"),
        check_vma=False,
    )
```

profile of v0, /device:TPU:0, one launch (start us, length us, event | category | flops | bytes accessed | tf_op | source)
XLA Modules:
  0.0 86.2 jit_solution(13903511328703697108)
XLA Ops:
  6.5 0.8 pad_maximum_fusion.24
  7.3 4.8 %collective-permute-start = (bf16[3,2,1024]{2,1,0:T(2,128)(2,1)S(1)}, bf16[3,2,1024]{2,1,0:T(2,128)(2,1)S(1)}, u32[]{:S(2)}, u32[]{:S(2)}) collective-permute-start(bf16[3,2,1024]{2,1,0:T(2,128)(2,1)S(1)} %pad_maximum_fusion.24), channel_id=1, source_target_pairs={{0,8},{8,16},{16,24},{1,9},{9,17},{17,25},{2,10},{10,18},{18,26},{... | collective-permute-start | bytes 36872 | tf_op jit(solution)/shard_map/ppermute | solution.py:13
  12.2 0.9 %fusion.53 = (f32[3,1,1024]{2,1,0:T(1,128)S(1)}, f32[3,1,1024]{2,1,0:T(1,128)S(1)}, f32[3,1,1024]{2,1,0:T(1,128)S(1)}) fusion(f32[3,3,1024]{2,1,0:T(4,128)} %param.13), kind=kLoop, calls=%fused_computation.116 | loop fusion | bytes 73728 | tf_op jit(solution)/shard_map/slice | solution.py:60
  13.5 1.3 %maximum_convert_fusion = f32[3,130,1024]{2,1,0:T(8,128)S(1)} fusion(bf16[1,128,1024]{2,1,0:T(8,128)(2,1)} %bitcast.47, bf16[1,128,1024]{2,1,0:T(8,128)(2,1)} %bitcast.49, bf16[1,128,1024]{2,1,0:T(8,128)(2,1)} %bitcast.51, bf16[3,2,1024]{2,1,0:T(2,128)(2,1)S(1)} %collective-permute-done), kind=kLoop, calls=%fused_computation.77 | loop fusion | flops 3194880 | bytes 2396160 | tf_op jit(solution)/shard_map/convert_element_type | solution.py:58
  14.9 0.5 fusion.48
  15.4 0.8 fusion.50
  16.2 9.6 %all-gather.1 = s32[4,1,128]{2,1,0:T(1,128)S(1)} all-gather(s32[1,1,128]{2,1,0:T(1,128)S(1)} %bitcast.71), channel_id=1, replica_groups=mesh['ctx'=4,'grp'=8] {'ctx'}, dimensions={0}, use_global_device_ids=true | all-gather | bytes 2560 | tf_op jit(solution)/shard_map/all_gather | solution.py:65
  25.8 0.6 slice.140
  27.1 17.9 %all-gather.4.cloned.1.call-done = bf16[1,512,1024]{2,1,0:T(8,128)(2,1)} async-done(((bf16[1,128,1024]{2,1,0:T(8,128)(2,1)}), bf16[1,512,1024]{2,1,0:T(8,128)(2,1)}) %all-gather.4.cloned.1.call-update) | async-done | bytes 1048592 | tf_op jit(solution)/shard_map/all_gather | solution.py:32
  45.0 16.9 %conditional.1 = (f32[128,1024]{1,0:T(8,128)S(1)}) conditional(s32[]{:T(128)} %convert_element_type.19, () %tuple.11, (s32[128]{0:T(128)S(1)}, s32[512]{0:T(512)S(1)}, s32[]{:T(128)}, bf16[1536]{0:T(1024)(128)(2,1)S(1)}, bf16[512,1024]{1,0:T(8,128)(2,1)}, /*index=5*/bf16[1536]{0:T(1024)(128)(2,1)S(1)}, bf16[1536]{0:T(1024)(128)(2,1)S(1)}, ...), branch_computations={%region_0.0_spmd, %region_1.2_spmd} | conditional | flops 135284224 | bytes 10332174 | solution.py:51
  45.8 0.4 reshape.35
  46.2 1.2 %convolution_dynamic-update-slice_fusion.7 = f32[128,1024]{0,1:T(8,128)S(1)} fusion(bf16[128,639]{1,0:T(8,128)(2,1)S(1)} %reshape.35, bf16[512,1024]{1,0:T(8,128)(2,1)} %get-tuple-element.39, s32[512]{0:T(512)S(1)} %get-tuple-element.36, s32[128]{0:T(128)S(1)} %get-tuple-element.35), kind=kOutput, calls=%fused_computation.7 | convolution fusion | flops 16908288 | bytes 330240 | tf_op jit(solution)/shard_map/cond/branch_1_fun/dot_general | solution.py:43
  48.0 1.2 %convolution_dynamic-update-slice_fusion.6 = f32[128,1024]{0,1:T(8,128)S(1)} fusion(f32[128,1024]{0,1:T(8,128)S(1)} %convolution_dynamic-update-slice_fusion.7, bf16[128,639]{1,0:T(8,128)(2,1)S(1)} %reshape.36, bf16[512,1024]{1,0:T(8,128)(2,1)} %get-tuple-element.39, s32[512]{0:T(512)S(1)} %get-tuple-element.36, s32[128]{0:T(128)S(1)} %get-tuple-element.35), kind=kOutput, calls=%fused_computation.6 | convolution fusion | flops 16908288 | bytes 330240 | tf_op jit(solution)/shard_map/cond/branch_1_fun/dot_general | solution.py:43
  50.3 1.2 %convolution_dynamic-update-slice_fusion.5 = f32[128,1024]{0,1:T(8,128)S(1)} fusion(f32[128,1024]{0,1:T(8,128)S(1)} %convolution_dynamic-update-slice_fusion.6, bf16[128,639]{1,0:T(8,128)(2,1)S(1)} %reshape.37, bf16[512,1024]{1,0:T(8,128)(2,1)} %get-tuple-element.39, s32[512]{0:T(512)S(1)} %get-tuple-element.36, s32[128]{0:T(128)S(1)} %get-tuple-element.35), kind=kOutput, calls=%fused_computation.5 | convolution fusion | flops 16908288 | bytes 330240 | tf_op jit(solution)/shard_map/cond/branch_1_fun/dot_general | solution.py:43
  51.7 0.4 reshape.38
  52.1 1.2 %convolution_dynamic-update-slice_fusion.4 = f32[128,1024]{0,1:T(8,128)S(1)} fusion(f32[128,1024]{0,1:T(8,128)S(1)} %convolution_dynamic-update-slice_fusion.5, bf16[128,639]{1,0:T(8,128)(2,1)S(1)} %reshape.38, bf16[512,1024]{1,0:T(8,128)(2,1)} %get-tuple-element.39, s32[512]{0:T(512)S(1)} %get-tuple-element.36, s32[128]{0:T(128)S(1)} %get-tuple-element.35), kind=kOutput, calls=%fused_computation.4 | convolution fusion | flops 16908288 | bytes 330240 | tf_op jit(solution)/shard_map/cond/branch_1_fun/dot_general | solution.py:43
  54.1 0.4 reshape.39
  54.5 1.2 %convolution_dynamic-update-slice_fusion.3 = f32[128,1024]{0,1:T(8,128)S(1)} fusion(f32[128,1024]{0,1:T(8,128)S(1)} %convolution_dynamic-update-slice_fusion.4, bf16[128,639]{1,0:T(8,128)(2,1)S(1)} %reshape.39, bf16[512,1024]{1,0:T(8,128)(2,1)} %get-tuple-element.39, s32[512]{0:T(512)S(1)} %get-tuple-element.36, s32[128]{0:T(128)S(1)} %get-tuple-element.35), kind=kOutput, calls=%fused_computation.3 | convolution fusion | flops 16908288 | bytes 330240 | tf_op jit(solution)/shard_map/cond/branch_1_fun/dot_general | solution.py:43
  56.3 1.2 %convolution_dynamic-update-slice_fusion.2 = f32[128,1024]{0,1:T(8,128)S(1)} fusion(f32[128,1024]{0,1:T(8,128)S(1)} %convolution_dynamic-update-slice_fusion.3, bf16[128,639]{1,0:T(8,128)(2,1)S(1)} %reshape.40, bf16[512,1024]{1,0:T(8,128)(2,1)} %get-tuple-element.39, s32[512]{0:T(512)S(1)} %get-tuple-element.36, s32[128]{0:T(128)S(1)} %get-tuple-element.35), kind=kOutput, calls=%fused_computation.2 | convolution fusion | flops 16908288 | bytes 330240 | tf_op jit(solution)/shard_map/cond/branch_1_fun/dot_general | solution.py:43
  58.7 1.2 %convolution_dynamic-update-slice_fusion.1 = f32[128,1024]{0,1:T(8,128)S(1)} fusion(f32[128,1024]{0,1:T(8,128)S(1)} %convolution_dynamic-update-slice_fusion.2, bf16[128,639]{1,0:T(8,128)(2,1)S(1)} %reshape.41, bf16[512,1024]{1,0:T(8,128)(2,1)} %get-tuple-element.39, s32[512]{0:T(512)S(1)} %get-tuple-element.36, s32[128]{0:T(128)S(1)} %get-tuple-element.35), kind=kOutput, calls=%fused_computation.1 | convolution fusion | flops 16908288 | bytes 330240 | tf_op jit(solution)/shard_map/cond/branch_1_fun/dot_general | solution.py:43
  60.1 0.4 reshape.42
  60.5 1.2 %convolution_dynamic-update-slice_fusion = f32[128,1024]{0,1:T(8,128)S(1)} fusion(f32[128,1024]{0,1:T(8,128)S(1)} %convolution_dynamic-update-slice_fusion.1, bf16[128,639]{1,0:T(8,128)(2,1)S(1)} %reshape.42, bf16[512,1024]{1,0:T(8,128)(2,1)} %get-tuple-element.39, s32[512]{0:T(512)S(1)} %get-tuple-element.36, s32[128]{0:T(128)S(1)} %get-tuple-element.35), kind=kOutput, calls=%fused_computation | convolution fusion | flops 16908288 | bytes 330240 | tf_op jit(solution)/shard_map/cond/branch_1_fun/dot_general | solution.py:43
  62.1 16.3 %psum.7 = f32[128]{0:T(128)S(1)} all-reduce(f32[128]{0:T(128)S(1)} %multiply_reduce_fusion), channel_id=1, replica_groups=mesh['ctx'=4,'grp'=8] {'grp'}, use_global_device_ids=true, to_apply=%region_3.4 | all-reduce | flops 128 | bytes 1024 | tf_op jit(solution)/shard_map/psum | solution.py:68
  78.5 0.9 %multiply_convert_fusion = bf16[128,1024]{1,0:T(8,128)(2,1)} fusion(f32[1024]{0:T(1024)S(1)} %copy-done.2, f32[128]{0:T(128)S(1)} %add_rsqrt_fusion, f32[128,1024]{1,0:T(8,128)S(1)} %get-tuple-element.47, f32[1024]{0:T(1024)S(1)} %copy-done.1, f32[3,128,1024]{2,1,0:T(8,128)S(1)} %fusion.48), kind=kLoop, calls=%fused_computation.84 | loop fusion | flops 1179648 | bytes 2368000 | tf_op jit(solution)/shard_map/convert_element_type | solution.py:70
  (68 shorter events, 6.2 us)
Async XLA Ops:
  6.5 38.5 %all-gather.4.cloned.1.call-start = ((), (), s32[]{:S(2)}) async-start(), calls=%async_computation | async-start | bytes 1310720 | tf_op jit(solution)/shard_map/all_gather | solution.py:32
  7.3 6.2 %collective-permute-start = (bf16[3,2,1024]{2,1,0:T(2,128)(2,1)S(1)}, bf16[3,2,1024]{2,1,0:T(2,128)(2,1)S(1)}, u32[]{:S(2)}, u32[]{:S(2)}) collective-permute-start(bf16[3,2,1024]{2,1,0:T(2,128)(2,1)S(1)} %pad_maximum_fusion.24), channel_id=1, source_target_pairs={{0,8},{8,16},{16,24},{1,9},{9,17},{17,25},{2,10},{10,18},{18,26},{... | collective-permute-start | bytes 36872 | tf_op jit(solution)/shard_map/ppermute | solution.py:13
  15.4 0.8 copy-start.3
  15.4 11.6 %copy-start = (bf16[8,512]{1,0:T(8,128)(2,1)S(1)}, bf16[8,512]{1,0:T(8,128)(2,1)}, u32[]{:S(2)}) copy-start(bf16[8,512]{1,0:T(8,128)(2,1)} %param.15) | copy-start | bytes 24580
  45.0 16.9 %copy-start.1 = (f32[1024]{0:T(1024)S(1)}, f32[1024]{0:T(1024)}, u32[]{:S(2)}) copy-start(f32[1024]{0:T(1024)} %param.14) | copy-start | bytes 12292
  61.9 16.6 %copy-start.2 = (f32[1024]{0:T(1024)S(1)}, f32[1024]{0:T(1024)}, u32[]{:S(2)}) copy-start(f32[1024]{0:T(1024)} %param.17) | copy-start | bytes 12292
Sparse Core Ops, SparseCore 0:
  16.3 28.6 all-gather.3
where the time goes:
time: 86.7 us; the launch traced here: 86.2 us
  blocking collectives  26 us (30%)
  waiting for transfers between devices  18.3 us (21%)
  between operations  14.1 us (16%)
  matrix products  9.61 us (11%)
  local copies, waits for them, and re-layouts  8.4 us (10%)
  starting transfers between devices  4.85 us (6%)
  other arithmetic  4.79 us (6%)
    all_gather x1, waiting for transfers between devices, token_conv(): piece = lax.all_gather(product_kv, 'ctx', axis=0, tiled=True)  17.9 us
    psum x1, blocking collectives, on_device(): squares = lax.psum(jnp.sum(gated * gated, axis=1), 'grp')  16.3 us
    all_gather x1, blocking collectives, on_device(): all_segs = lax.all_gather(segments, 'ctx', axis=0, tiled=True)  9.63 us
    dot_general x8, matrix products, work(): jnp.dot(matrix, piece[:, group * GW:(group + 1) * GW], preferred_element_...  9.61 us
    ppermute x1, starting transfers between devices, shifted(): return lax.ppermute(value, axis, pairs)  4.84 us
    reshape x8, local copies, waits for them, and re-layouts, band_rect(): tiled = jnp.tile(flipped, rows)[:rows * length].reshape(rows, length)  3.31 us
  transfers between devices with their start and end apart: 2, of which 2 were waited for; matrix products, arithmetic and copies ran while one was open for 2% of the time, Pallas kernels for 0%

commit v1 on v0

v1 whole, which is shorter than its diff:
```python
import functools

import jax
import jax.numpy as jnp
from jax import lax
from jax.experimental import pallas as pl
from jax.experimental.pallas import tpu as pltpu
from jax.sharding import PartitionSpec as P

D = 8192
GW = 128
F32 = jnp.float32
BF16 = jnp.bfloat16
MESH = pl.DeviceIdType.MESH


def lagged(x, by, rows):
    return jnp.where(rows >= by, pltpu.roll(x, by, 0), 0.0)


def kernel(
    n, m, groups,
    q_hbm, k_hbm, v_hbm, fir, skip, taps, seg, gain, out,
    qbuf, kbuf, vbuf, own, slots, aux, fixes, mats, acc, fq, sqs,
    in_sem, aux_send, aux_recv, kv_send, kv_recv, fwd_send, sq_send, sq_recv,
):
    me, gi = lax.axis_index("ctx"), lax.axis_index("grp")
    tokens, width = qbuf.shape
    far = n - 2
    relay = n == 4

    barrier = pltpu.get_barrier_semaphore()
    for d in range(1, n):
        pl.semaphore_signal(barrier, inc=1, device_id={"ctx": lax.rem(me + d, n)}, device_id_type=MESH)
    for e in range(1, m):
        pl.semaphore_signal(barrier, inc=1, device_id={"grp": lax.rem(gi + e, m)}, device_id_type=MESH)
    loads = [
        pltpu.make_async_copy(src, dst, in_sem.at[i])
        for i, (src, dst) in enumerate(((k_hbm, kbuf), (v_hbm, vbuf), (q_hbm, qbuf)))
    ]
    for load in loads:
        load.start()

    def aux_copy(d, peer):
        return pltpu.make_async_remote_copy(
            src_ref=aux.at[0], dst_ref=aux.at[d], send_sem=aux_send.at[d - 1], recv_sem=aux_recv.at[d - 1],
            device_id={"ctx": peer}, device_id_type=MESH)

    def kv_copy(d, g, peer):
        return pltpu.make_async_remote_copy(
            src_ref=own.at[g], dst_ref=slots.at[d - 1, g], send_sem=kv_send.at[d - 1, g],
            recv_sem=kv_recv.at[d - 1, g], device_id={"ctx": peer}, device_id_type=MESH)

    def forward(g):
        return pltpu.make_async_remote_copy(
            src_ref=slots.at[1, g], dst_ref=slots.at[0, g], send_sem=fwd_send.at[g],
            recv_sem=kv_recv.at[0, g], device_id={"ctx": 2}, device_id_type=MESH)

    def sends(d):
        there = me + d < n
        return there & (me != 1) if relay and d == 1 else there

    rows = lax.broadcasted_iota(jnp.int32, (tokens, GW), 0)
    cols = lax.broadcasted_iota(jnp.int32, (tokens, GW), 1)
    row8 = lax.broadcasted_iota(jnp.int32, (8, width), 0)
    for load in loads:
        load.wait()

    def last8(ref):
        return ref[tokens - 16 :, :].astype(F32)[8:]

    def first8(ref):
        return ref[:16, :].astype(F32)[:8]

    seg_f = seg[...].astype(F32)
    seg_tile = jnp.concatenate([jnp.broadcast_to(seg_f, (8, GW))] * groups, axis=1)
    upper = jnp.where(
        row8 < 4,
        jnp.where(row8 < 2, pltpu.roll(last8(kbuf), 2, 0), pltpu.roll(first8(kbuf), 2, 0)),
        jnp.where(row8 < 6, pltpu.roll(last8(vbuf), 6, 0), pltpu.roll(first8(vbuf), 6, 0)))
    lower = jnp.where(row8 < 2, pltpu.roll(last8(qbuf), 2, 0), seg_tile)
    aux[0] = jnp.concatenate([upper, lower], axis=0).astype(BF16)

    pl.semaphore_wait(barrier, n - 1 + m - 1)
    for d in range(1, n):
        @pl.when(me + d < n)
        def _():
            aux_copy(d, me + d).start()

    for g in range(groups):
        lane = slice(g * GW, (g + 1) * GW)

        def filtered(ref, a):
            x = ref[:, lane].astype(F32)
            return (fir[a, 0:1, lane] * x + fir[a, 1:2, lane] * lagged(x, 1, rows)
                    + fir[a, 2:3, lane] * lagged(x, 2, rows))

        own[g] = (filtered(kbuf, 1) * filtered(vbuf, 2)).astype(BF16)
        for d in range(1, far + 1):
            @pl.when(sends(d))
            def _():
                kv_copy(d, g, me + d).start()

    for d in range(1, n):
        @pl.when(me >= d)
        def _():
            aux_copy(d, me - d).wait_recv()

    for d in range(far + 1):
        @pl.when(me - d >= 1)
        def _():
            before, after = aux[d + 1].astype(F32)[:8], aux[d].astype(F32)[:8]
            edge = jnp.where(lax.rem(row8, 4) < 2, before, after)
            tap = [jnp.where(row8 < 4, fir[1, i : i + 1, :], fir[2, i : i + 1, :]) for i in range(3)]
            both = tap[0] * edge + tap[1] * pltpu.roll(edge, 1, 0) + tap[2] * pltpu.roll(edge, 2, 0)
            fixes[d] = pltpu.roll(both * pltpu.roll(both, 4, 0), 6, 0)

    def block_of(ref, d, g):
        lane = slice(g * GW, (g + 1) * GW)
        whole = ref[...]
        top = whole[:16].astype(F32)
        limit = jnp.where(me - d >= 1, 2, 0)
        head = jnp.where(row8[:, :GW] < limit, fixes[d, :, lane], top[:8])
        return jnp.concatenate([jnp.concatenate([head, top[8:]], axis=0).astype(BF16), whole[16:]], axis=0)

    flip = (rows + cols == GW - 1).astype(BF16)
    target = jnp.broadcast_to(seg_f, (tokens, GW)).T
    same = [aux[d].astype(F32)[10:11, :GW] == target for d in range(far + 1)]
    same[0] = same[0] & (cols <= rows)
    for d in range(far + 1):
        back = jnp.dot(taps[:, d * GW : (d + 1) * GW], flip, preferred_element_type=F32)
        for g in range(groups):
            turned = pltpu.roll(jnp.broadcast_to(back[g : g + 1], (tokens, GW)), 1, 1, stride=1, stride_axis=0)
            if d < far:
                mats[d + 1, g] = jnp.where(same[d + 1] & (cols > rows), turned, 0.0).astype(BF16)
            if d == 0:
                mats[0, g] = jnp.where(same[0], turned, 0.0).astype(BF16)
            else:
                mats[d, g] += jnp.where(same[d] & (cols <= rows), turned, 0.0).astype(BF16)

    for g in range(groups):
        lane = slice(g * GW, (g + 1) * GW)
        block = block_of(own.at[g], 0, g)
        acc[g] = jnp.dot(mats[0, g], block, preferred_element_type=F32) + skip[:, lane] * block.astype(F32)
        x = qbuf[:, lane].astype(F32)
        halo = jnp.where(me >= 1, aux[1, :, lane].astype(F32), 0.0)
        one = jnp.where(rows < 1, halo[9:10], pltpu.roll(x, 1, 0))
        two = jnp.where(rows < 1, halo[8:9], jnp.where(rows < 2, halo[9:10], pltpu.roll(x, 2, 0)))
        fq[g] = fir[0, 0:1, lane] * x + fir[0, 1:2, lane] * one + fir[0, 2:3, lane] * two

    squares = jnp.zeros((tokens, GW), F32)
    for g in range(groups):
        for d in range(far, 0, -1):
            @pl.when(me >= d)
            def _():
                kv_copy(d, g, me - d).wait_recv()
                if relay and d == 2:
                    @pl.when(me == 3)
                    def _():
                        forward(g).start()
                acc[g] += jnp.dot(mats[d, g], block_of(slots.at[d - 1, g], d, g), preferred_element_type=F32)
        gated = fq[g] * acc[g]
        acc[g] = gated
        squares += gated * gated

    sqs[0] = jnp.sum(squares.T.reshape(GW // 8, 8, tokens), axis=0)

    def sq_copy(e, peer):
        return pltpu.make_async_remote_copy(
            src_ref=sqs.at[0], dst_ref=sqs.at[e], send_sem=sq_send.at[e - 1], recv_sem=sq_recv.at[e - 1],
            device_id={"grp": peer}, device_id_type=MESH)

    for e in range(1, m):
        sq_copy(e, lax.rem(gi + e, m)).start()
    for e in range(1, m):
        sq_copy(e, lax.rem(gi + m - e, m)).wait_recv()
    total = sqs[0]
    for e in range(1, m):
        total += sqs[e]
    scale = lax.rsqrt(jnp.sum(total, axis=0, keepdims=True) / D + 1e-06)
    scale = jnp.broadcast_to(scale, (GW, tokens)).T
    for g in range(groups):
        lane = slice(g * GW, (g + 1) * GW)
        out[:, lane] = (acc[g] * scale * gain[:, lane]).astype(BF16)

    for e in range(1, m):
        sq_copy(e, lax.rem(gi + e, m)).wait_send()
    for d in range(1, n):
        @pl.when(me + d < n)
        def _():
            aux_copy(d, me + d).wait_send()
    for d in range(1, far + 1):
        @pl.when(sends(d))
        def _():
            for g in range(groups):
                kv_copy(d, g, me + d).wait_send()
    if relay:
        @pl.when(me == 3)
        def _():
            for g in range(groups):
                forward(g).wait_send()


def on_device(n, m, q_in, k_in, v_in, fir, skip, taps, segments, gain):
    tokens, width = q_in.shape
    groups = width // GW
    far = n - 2
    vmem = pl.BlockSpec(memory_space=pltpu.VMEM)
    hbm = pl.BlockSpec(memory_space=pl.ANY)
    block = (groups, tokens, GW)
    dma = pltpu.SemaphoreType.DMA
    return pl.pallas_call(
        functools.partial(kernel, n, m, groups),
        out_shape=jax.ShapeDtypeStruct((tokens, width), BF16),
        in_specs=[hbm] * 3 + [vmem] * 5,
        out_specs=vmem,
        scratch_shapes=[
            pltpu.VMEM((tokens, width), BF16),
            pltpu.VMEM((tokens, width), BF16),
            pltpu.VMEM((tokens, width), BF16),
            pltpu.VMEM(block, BF16),
            pltpu.VMEM((far,) + block, BF16),
            pltpu.VMEM((n, 16, width), BF16),
            pltpu.VMEM((far + 1, 8, width), F32),
            pltpu.VMEM((far + 1,) + block, BF16),
            pltpu.VMEM(block, F32),
            pltpu.VMEM(block, F32),
            pltpu.VMEM((m, 8, tokens), F32),
            dma((3,)),
            dma((n - 1,)),
            dma((n - 1,)),
            dma((far, groups)),
            dma((far, groups)),
            dma((groups,)),
            dma((m - 1,)),
            dma((m - 1,)),
        ],
        compiler_params=pltpu.CompilerParams(
            collective_id=0, has_side_effects=True, vmem_limit_bytes=40 * 1024 * 1024
        ),
        cost_estimate=pl.CostEstimate(
            flops=2 * tokens * tokens * width * (far + 1), bytes_accessed=8 * tokens * width, transcendentals=0
        ),
        name="mixer",
    )(q_in, k_in, v_in, fir, skip[None, :], taps, segments[None, :], gain[None, :])


def solution(mesh):
    return jax.shard_map(
        functools.partial(on_device, mesh.shape["ctx"], mesh.shape["grp"]),
        mesh=mesh,
        in_specs=(
            P("ctx", "grp"),
            P("ctx", "grp"),
            P("ctx", "grp"),
            P(None, None, "grp"),
            P("grp"),
            P("grp", None),
            P("ctx"),
            P("grp"),
        ),
        out_specs=P("ctx", "grp"),
        check_vma=False,
    )
```

time: 86.7 us -> 26.5 us (0.31)
  the two profiles are of different devices: /device:TPU:0 before, /device:TPU:5 now
where the time goes in v1:
time: 26.5 us; the launch traced here: 26.2 us
  Pallas kernels  19.7 us (74%)
  local copies, waits for them, and re-layouts  6.42 us (24%)
    pallas_call x1, Pallas kernels, on_device(): pl.pallas_call(functools.partial(kernel, n, m, groups), out_shape=jax.Sha...  19.7 us
    unnamed x17, local copies, waits for them, and re-layouts  6.42 us

profile of v1, /device:TPU:5, one launch (start us, length us, event | category | flops | bytes accessed | tf_op | source)
XLA Modules:
  0.0 26.2 jit_solution(14104731319539797895)
XLA Ops:
  0.0 0.0 copy-start.5
  0.0 0.0 copy-start.7
  0.0 0.7 %copy-done.5 = f32[1024]{0:T(1024)S(1)} copy-done((f32[1024]{0:T(1024)S(1)}, f32[1024]{0:T(1024)}, u32[]{:S(2)}) %copy-start.5) | copy-done | bytes 4120
  0.7 0.0 copy-done.7
  0.7 0.0 copy-start
  0.7 0.9 %copy-done = bf16[128,1024]{1,0:T(8,128)(2,1)S(1)} copy-done((bf16[128,1024]{1,0:T(8,128)(2,1)S(1)}, bf16[128,1024]{1,0:T(8,128)(2,1)}, u32[]{:S(2)}) %copy-start) | copy-done | bytes 262168
  1.6 0.0 copy-start.1
  1.6 0.9 %copy-done.1 = bf16[128,1024]{1,0:T(8,128)(2,1)S(1)} copy-done((bf16[128,1024]{1,0:T(8,128)(2,1)S(1)}, bf16[128,1024]{1,0:T(8,128)(2,1)}, u32[]{:S(2)}) %copy-start.1) | copy-done | bytes 262168
  2.6 0.0 copy-start.2
  2.6 0.9 %copy-done.2 = bf16[128,1024]{1,0:T(8,128)(2,1)S(1)} copy-done((bf16[128,1024]{1,0:T(8,128)(2,1)S(1)}, bf16[128,1024]{1,0:T(8,128)(2,1)}, u32[]{:S(2)}) %copy-start.2) | copy-done | bytes 262168
  3.5 0.0 copy-start.3
  3.5 0.8 %copy-done.3 = f32[3,3,1024]{2,1,0:T(4,128)S(1)} copy-done((f32[3,3,1024]{2,1,0:T(4,128)S(1)}, f32[3,3,1024]{2,1,0:T(4,128)}, u32[]{:S(2)}) %copy-start.3) | copy-done | bytes 36888
  4.3 0.0 copy-start.4
  4.3 0.7 %copy-done.4 = bf16[8,512]{1,0:T(8,128)(2,1)S(1)} copy-done((bf16[8,512]{1,0:T(8,128)(2,1)S(1)}, bf16[8,512]{1,0:T(8,128)(2,1)}, u32[]{:S(2)}) %copy-start.4) | copy-done | bytes 8216
  5.0 0.0 copy-start.6
  5.0 0.7 %copy-done.6 = f32[1024]{0:T(1024)S(1)} copy-done((f32[1024]{0:T(1024)S(1)}, f32[1024]{0:T(1024)}, u32[]{:S(2)}) %copy-start.6) | copy-done | bytes 4120
  5.7 19.7 %mixer.1 = bf16[128,1024]{1,0:T(8,128)(2,1)S(1)} custom-call(bf16[128,1024]{1,0:T(8,128)(2,1)S(1)} %copy-done, bf16[128,1024]{1,0:T(8,128)(2,1)S(1)} %copy-done.1, bf16[128,1024]{1,0:T(8,128)(2,1)S(1)} %copy-done.2, f32[3,3,1024]{2,1,0:T(4,128)S(1)} %copy-done.3, f32[1,1024]{1,0:T(1,128)S(1)} %bitcast.3, bf16[8,512]{1,0:T(8,128)(2,1)S(1)} %copy-done.4, ...), custom_call_target="tpu_custom_call" | custom-call | flops 100663296 | bytes 1048576 | tf_op jit(solution)/shard_map/mixer/pallas_call | solution.py:212
  25.5 0.7 %copy.10 = bf16[128,1024]{1,0:T(8,128)(2,1)} copy(bf16[128,1024]{1,0:T(8,128)(2,1)S(1)} %mixer.1) | data formatting | bytes 524288
Async XLA Ops:
  0.0 0.7 %copy-start.5 = (f32[1024]{0:T(1024)S(1)}, f32[1024]{0:T(1024)}, u32[]{:S(2)}) copy-start(f32[1024]{0:T(1024)} %param.12) | copy-start | bytes 12292
  0.0 0.7 %copy-start.7 = (s32[128]{0:T(128)S(1)}, s32[128]{0:T(128)}, u32[]{:S(2)}) copy-start(s32[128]{0:T(128)} %param.14) | copy-start | bytes 1540
  0.7 1.0 %copy-start = (bf16[128,1024]{1,0:T(8,128)(2,1)S(1)}, bf16[128,1024]{1,0:T(8,128)(2,1)}, u32[]{:S(2)}) copy-start(bf16[128,1024]{1,0:T(8,128)(2,1)} %q_hbm.1) | copy-start | bytes 786436
  1.6 0.9 %copy-start.1 = (bf16[128,1024]{1,0:T(8,128)(2,1)S(1)}, bf16[128,1024]{1,0:T(8,128)(2,1)}, u32[]{:S(2)}) copy-start(bf16[128,1024]{1,0:T(8,128)(2,1)} %k_hbm.1) | copy-start | bytes 786436
  2.6 0.9 %copy-start.2 = (bf16[128,1024]{1,0:T(8,128)(2,1)S(1)}, bf16[128,1024]{1,0:T(8,128)(2,1)}, u32[]{:S(2)}) copy-start(bf16[128,1024]{1,0:T(8,128)(2,1)} %v_hbm.1) | copy-start | bytes 786436
  3.5 0.8 %copy-start.3 = (f32[3,3,1024]{2,1,0:T(4,128)S(1)}, f32[3,3,1024]{2,1,0:T(4,128)}, u32[]{:S(2)}) copy-start(f32[3,3,1024]{2,1,0:T(4,128)} %fir.1) | copy-start | bytes 110596
  4.3 0.7 %copy-start.4 = (bf16[8,512]{1,0:T(8,128)(2,1)S(1)}, bf16[8,512]{1,0:T(8,128)(2,1)}, u32[]{:S(2)}) copy-start(bf16[8,512]{1,0:T(8,128)(2,1)} %taps.1) | copy-start | bytes 24580
  5.0 0.7 %copy-start.6 = (f32[1024]{0:T(1024)S(1)}, f32[1024]{0:T(1024)}, u32[]{:S(2)}) copy-start(f32[1024]{0:T(1024)} %param.15) | copy-start | bytes 12292

commit v2 on v1

--- a/solution.py
+++ b/solution.py
@@ -20,8 +20,8 @@
 
 def kernel(
     n, m, groups,
-    q_hbm, k_hbm, v_hbm, fir, skip, taps, seg, gain, out,
-    qbuf, kbuf, vbuf, own, slots, aux, fixes, mats, acc, fq, sqs,
+    q_hbm, k_hbm, v_hbm, fir_hbm, skip_hbm, taps_hbm, seg_hbm, gain_hbm, out,
+    qbuf, kbuf, vbuf, fir, skip, taps, seg, gain, own, slots, aux, fixes, mats, acc, sqs,
     in_sem, aux_send, aux_recv, kv_send, kv_recv, fwd_send, sq_send, sq_recv,
 ):
     me, gi = lax.axis_index("ctx"), lax.axis_index("grp")
@@ -29,18 +29,18 @@
     far = n - 2
     relay = n == 4
 
-    barrier = pltpu.get_barrier_semaphore()
-    for d in range(1, n):
-        pl.semaphore_signal(barrier, inc=1, device_id={"ctx": lax.rem(me + d, n)}, device_id_type=MESH)
-    for e in range(1, m):
-        pl.semaphore_signal(barrier, inc=1, device_id={"grp": lax.rem(gi + e, m)}, device_id_type=MESH)
-    loads = [
-        pltpu.make_async_copy(src, dst, in_sem.at[i])
-        for i, (src, dst) in enumerate(((k_hbm, kbuf), (v_hbm, vbuf), (q_hbm, qbuf)))
-    ]
+    pairs = (
+        (k_hbm, kbuf), (v_hbm, vbuf), (q_hbm, qbuf), (fir_hbm, fir),
+        (seg_hbm, seg), (taps_hbm, taps), (skip_hbm, skip), (gain_hbm, gain),
+    )
+    loads = [pltpu.make_async_copy(src, dst, in_sem.at[i]) for i, (src, dst) in enumerate(pairs)]
     for load in loads:
         load.start()
-
+    barrier = pltpu.get_barrier_semaphore()
+    for d in range(1, n):
+        pl.semaphore_signal(barrier, inc=1, device_id={"ctx": lax.rem(me + d, n)}, device_id_type=MESH)
+    for e in range(1, m):
+        pl.semaphore_signal(barrier, inc=1, device_id={"grp": lax.rem(gi + e, m)}, device_id_type=MESH)
     def aux_copy(d, peer):
         return pltpu.make_async_remote_copy(
             src_ref=aux.at[0], dst_ref=aux.at[d], send_sem=aux_send.at[d - 1], recv_sem=aux_recv.at[d - 1],
@@ -81,13 +81,7 @@
     lower = jnp.where(row8 < 2, pltpu.roll(last8(qbuf), 2, 0), seg_tile)
     aux[0] = jnp.concatenate([upper, lower], axis=0).astype(BF16)
 
-    pl.semaphore_wait(barrier, n - 1 + m - 1)
-    for d in range(1, n):
-        @pl.when(me + d < n)
-        def _():
-            aux_copy(d, me + d).start()
-
-    for g in range(groups):
+    def product(g):
         lane = slice(g * GW, (g + 1) * GW)
 
         def filtered(ref, a):
@@ -96,10 +90,23 @@
                     + fir[a, 2:3, lane] * lagged(x, 2, rows))
 
         own[g] = (filtered(kbuf, 1) * filtered(vbuf, 2)).astype(BF16)
+
+    def send_chunk(g):
         for d in range(1, far + 1):
             @pl.when(sends(d))
             def _():
                 kv_copy(d, g, me + d).start()
+
+    product(0)
+    pl.semaphore_wait(barrier, n - 1 + m - 1)
+    for d in range(1, n):
+        @pl.when(me + d < n)
+        def _():
+            aux_copy(d, me + d).start()
+    send_chunk(0)
+    for g in range(1, groups):
+        product(g)
+        send_chunk(g)
 
     for d in range(1, n):
         @pl.when(me >= d)
@@ -125,31 +132,29 @@
 
     flip = (rows + cols == GW - 1).astype(BF16)
     target = jnp.broadcast_to(seg_f, (tokens, GW)).T
-    same = [aux[d].astype(F32)[10:11, :GW] == target for d in range(far + 1)]
-    same[0] = same[0] & (cols <= rows)
-    for d in range(far + 1):
-        back = jnp.dot(taps[:, d * GW : (d + 1) * GW], flip, preferred_element_type=F32)
-        for g in range(groups):
-            turned = pltpu.roll(jnp.broadcast_to(back[g : g + 1], (tokens, GW)), 1, 1, stride=1, stride_axis=0)
-            if d < far:
-                mats[d + 1, g] = jnp.where(same[d + 1] & (cols > rows), turned, 0.0).astype(BF16)
-            if d == 0:
-                mats[0, g] = jnp.where(same[0], turned, 0.0).astype(BF16)
-            else:
-                mats[d, g] += jnp.where(same[d] & (cols <= rows), turned, 0.0).astype(BF16)
-
+    back = [
+        jnp.dot(taps[:, d * GW : (d + 1) * GW], flip, preferred_element_type=F32) for d in range(far + 1)
+    ]
+
+    def matrices(g):
+        nearer = 0.0
+        for d in range(far + 1):
+            turned = pltpu.roll(jnp.broadcast_to(back[d][g : g + 1], (tokens, GW)), 1, 1, stride=1, stride_axis=0)
+            same = aux[d].astype(F32)[10:11, :GW] == target
+            mats[d] = jnp.where(same, jnp.where(cols <= rows, turned, nearer), 0.0).astype(BF16)
+            nearer = turned
+
+    squares = jnp.zeros((tokens, GW), F32)
     for g in range(groups):
         lane = slice(g * GW, (g + 1) * GW)
+        matrices(g)
         block = block_of(own.at[g], 0, g)
-        acc[g] = jnp.dot(mats[0, g], block, preferred_element_type=F32) + skip[:, lane] * block.astype(F32)
+        acc[g] = jnp.dot(mats[0], block, preferred_element_type=F32) + skip[:, lane] * block.astype(F32)
         x = qbuf[:, lane].astype(F32)
         halo = jnp.where(me >= 1, aux[1, :, lane].astype(F32), 0.0)
         one = jnp.where(rows < 1, halo[9:10], pltpu.roll(x, 1, 0))
         two = jnp.where(rows < 1, halo[8:9], jnp.where(rows < 2, halo[9:10], pltpu.roll(x, 2, 0)))
-        fq[g] = fir[0, 0:1, lane] * x + fir[0, 1:2, lane] * one + fir[0, 2:3, lane] * two
-
-    squares = jnp.zeros((tokens, GW), F32)
-    for g in range(groups):
+        query = fir[0, 0:1, lane] * x + fir[0, 1:2, lane] * one + fir[0, 2:3, lane] * two
         for d in range(far, 0, -1):
             @pl.when(me >= d)
             def _():
@@ -158,8 +163,8 @@
                     @pl.when(me == 3)
                     def _():
                         forward(g).start()
-                acc[g] += jnp.dot(mats[d, g], block_of(slots.at[d - 1, g], d, g), preferred_element_type=F32)
-        gated = fq[g] * acc[g]
+                acc[g] += jnp.dot(mats[d], block_of(slots.at[d - 1, g], d, g), preferred_element_type=F32)
+        gated = query * acc[g]
         acc[g] = gated
         squares += gated * gated
 
@@ -206,27 +211,31 @@
     groups = width // GW
     far = n - 2
     vmem = pl.BlockSpec(memory_space=pltpu.VMEM)
-    hbm = pl.BlockSpec(memory_space=pl.ANY)
+    hbm = pl.BlockSpec(memory_space=pltpu.HBM)
     block = (groups, tokens, GW)
     dma = pltpu.SemaphoreType.DMA
     return pl.pallas_call(
         functools.partial(kernel, n, m, groups),
         out_shape=jax.ShapeDtypeStruct((tokens, width), BF16),
-        in_specs=[hbm] * 3 + [vmem] * 5,
+        in_specs=[hbm] * 8,
         out_specs=vmem,
         scratch_shapes=[
             pltpu.VMEM((tokens, width), BF16),
             pltpu.VMEM((tokens, width), BF16),
             pltpu.VMEM((tokens, width), BF16),
+            pltpu.VMEM(fir.shape, F32),
+            pltpu.VMEM((1, width), F32),
+            pltpu.VMEM(taps.shape, BF16),
+            pltpu.VMEM((1, tokens), jnp.int32),
+            pltpu.VMEM((1, width), F32),
             pltpu.VMEM(block, BF16),
             pltpu.VMEM((far,) + block, BF16),
             pltpu.VMEM((n, 16, width), BF16),
             pltpu.VMEM((far + 1, 8, width), F32),
-            pltpu.VMEM((far + 1,) + block, BF16),
-            pltpu.VMEM(block, F32),
+            pltpu.VMEM((far + 1, tokens, GW), BF16),
             pltpu.VMEM(block, F32),
             pltpu.VMEM((m, 8, tokens), F32),
-            dma((3,)),
+            dma((8,)),
             dma((n - 1,)),
             dma((n - 1,)),
             dma((far, groups)),
@@ -236,7 +245,7 @@
             dma((m - 1,)),
         ],
         compiler_params=pltpu.CompilerParams(
-            collective_id=0, has_side_effects=True, vmem_limit_bytes=40 * 1024 * 1024
+            collective_id=0, has_side_effects=True, vmem_limit_bytes=63 * 1024 * 1024
         ),
         cost_estimate=pl.CostEstimate(
             flops=2 * tokens * tokens * width * (far + 1), bytes_accessed=8 * tokens * width, transcendentals=0

time: 26.5 us -> 22.9 us (0.86)
  local copies, waits for them, and re-layouts: 6.42 us -> 1.67 us
  Pallas kernels: 19.7 us -> 21.1 us
    unnamed x17 -> x1, local copies, waits for them, and re-layouts: 6.42 us -> 1.67 us
    pallas_call x1, Pallas kernels: 19.7 us -> 21.1 us  [on_device(): pl.pallas_call(functools.partial(kernel, n, m, groups), out_shape=jax.Sha...]
where the time goes in v2:
time: 22.9 us; the launch traced here: 22.8 us
  Pallas kernels  21.1 us (92%)
  local copies, waits for them, and re-layouts  1.67 us (7%)
    pallas_call x1, Pallas kernels, on_device(): pl.pallas_call(functools.partial(kernel, n, m, groups), out_shape=jax.Sha...  21.1 us
    unnamed x1, local copies, waits for them, and re-layouts  1.67 us

profile of v2, /device:TPU:5, one launch (start us, length us, event | category | flops | bytes accessed | tf_op | source)
XLA Modules:
  0.0 22.8 jit_solution(8698255205532811970)
XLA Ops:
  0.0 21.1 %mixer.1 = bf16[128,1024]{1,0:T(8,128)(2,1)} custom-call(bf16[128,1024]{1,0:T(8,128)(2,1)} %q_hbm.1, bf16[128,1024]{1,0:T(8,128)(2,1)} %k_hbm.1, bf16[128,1024]{1,0:T(8,128)(2,1)} %v_hbm.1, f32[3,3,1024]{2,1,0:T(4,128)} %fir_hbm.1, f32[1,1024]{1,0:T(1,128)} %bitcast.3, bf16[8,512]{1,0:T(8,128)(2,1)} %taps_hbm.1, s32[1,128]{1,0:T(1,128)} %bitcast.5, ...), custom_call_target="tpu_custom_call" | custom-call | flops 100663296 | bytes 1048576 | tf_op jit(solution)/shard_map/mixer/pallas_call | solution.py:217
  21.1 1.7 %copy.10 = bf16[128,1024]{1,0:T(8,128)(2,1)} copy(bf16[128,1024]{1,0:T(8,128)(2,1)} %mixer.1) | data formatting | bytes 524288

commit v3 on v2

--- a/solution.py
+++ b/solution.py
@@ -28,6 +28,8 @@
     tokens, width = qbuf.shape
     far = n - 2
     relay = n == 4
+    relayed = groups - max(1, groups // 4)
+    ahead = 2
 
     pairs = (
         (k_hbm, kbuf), (v_hbm, vbuf), (q_hbm, qbuf), (fir_hbm, fir),
@@ -56,9 +58,16 @@
             src_ref=slots.at[1, g], dst_ref=slots.at[0, g], send_sem=fwd_send.at[g],
             recv_sem=kv_recv.at[0, g], device_id={"ctx": 2}, device_id_type=MESH)
 
-    def sends(d):
+    def sends(d, g):
         there = me + d < n
-        return there & (me != 1) if relay and d == 1 else there
+        return there & (me != 1) if relay and d == 1 and g < relayed else there
+
+    def pass_on(g):
+        if relay and g < relayed:
+            @pl.when(me == 3)
+            def _():
+                kv_copy(2, g, 1).wait_recv()
+                forward(g).start()
 
     rows = lax.broadcasted_iota(jnp.int32, (tokens, GW), 0)
     cols = lax.broadcasted_iota(jnp.int32, (tokens, GW), 1)
@@ -93,7 +102,7 @@
 
     def send_chunk(g):
         for d in range(1, far + 1):
-            @pl.when(sends(d))
+            @pl.when(sends(d, g))
             def _():
                 kv_copy(d, g, me + d).start()
 
@@ -145,8 +154,11 @@
             nearer = turned
 
     squares = jnp.zeros((tokens, GW), F32)
+    for g in range(ahead):
+        pass_on(g)
     for g in range(groups):
         lane = slice(g * GW, (g + 1) * GW)
+        pass_on(g + ahead)
         matrices(g)
         block = block_of(own.at[g], 0, g)
         acc[g] = jnp.dot(mats[0], block, preferred_element_type=F32) + skip[:, lane] * block.astype(F32)
@@ -158,11 +170,12 @@
         for d in range(far, 0, -1):
             @pl.when(me >= d)
             def _():
-                kv_copy(d, g, me - d).wait_recv()
-                if relay and d == 2:
-                    @pl.when(me == 3)
+                if relay and d == 2 and g < relayed:
+                    @pl.when(me == 2)
                     def _():
-                        forward(g).start()
+                        kv_copy(d, g, me - d).wait_recv()
+                else:
+                    kv_copy(d, g, me - d).wait_recv()
                 acc[g] += jnp.dot(mats[d], block_of(slots.at[d - 1, g], d, g), preferred_element_type=F32)
         gated = query * acc[g]
         acc[g] = gated
@@ -195,14 +208,14 @@
         def _():
             aux_copy(d, me + d).wait_send()
     for d in range(1, far + 1):
-        @pl.when(sends(d))
-        def _():
-            for g in range(groups):
+        for g in range(groups):
+            @pl.when(sends(d, g))
+            def _():
                 kv_copy(d, g, me + d).wait_send()
     if relay:
         @pl.when(me == 3)
         def _():
-            for g in range(groups):
+            for g in range(relayed):
                 forward(g).wait_send()
 
 
@@ -216,7 +229,7 @@
     dma = pltpu.SemaphoreType.DMA
     return pl.pallas_call(
         functools.partial(kernel, n, m, groups),
-        out_shape=jax.ShapeDtypeStruct((tokens, width), BF16),
+        out_shape=pltpu.VMEM((tokens, width), BF16),
         in_specs=[hbm] * 8,
         out_specs=vmem,
         scratch_shapes=[
@@ -245,13 +258,16 @@
             dma((m - 1,)),
         ],
         compiler_params=pltpu.CompilerParams(
-            collective_id=0, has_side_effects=True, vmem_limit_bytes=63 * 1024 * 1024
+            collective_id=0, has_side_effects=True, vmem_limit_bytes=40 * 1024 * 1024
         ),
         cost_estimate=pl.CostEstimate(
             flops=2 * tokens * tokens * width * (far + 1), bytes_accessed=8 * tokens * width, transcendentals=0
         ),
         name="mixer",
-    )(q_in, k_in, v_in, fir, skip[None, :], taps, segments[None, :], gain[None, :])
+    )(*[
+        pltpu.with_memory_space_constraint(x, pltpu.HBM)
+        for x in (q_in, k_in, v_in, fir, skip[None, :], taps, segments[None, :], gain[None, :])
+    ])
 
 
 def solution(mesh):

time: 22.9 us -> 20.7 us (0.904)
  Pallas kernels: 21.1 us -> 19.8 us
  local copies, waits for them, and re-layouts: 1.67 us -> 0.71 us
    pallas_call x1, Pallas kernels: 21.1 us -> 19.8 us  [on_device(): pl.pallas_call(functools.partial(kernel, n, m, groups), out_shape=pltpu.V...]
    unnamed x1, local copies, waits for them, and re-layouts: 1.67 us -> 0.71 us
where the time goes in v3:
time: 20.7 us; the launch traced here: 20.5 us
  Pallas kernels  19.8 us (96%)
  local copies, waits for them, and re-layouts  0.71 us (3%)
    pallas_call x1, Pallas kernels, on_device(): pl.pallas_call(functools.partial(kernel, n, m, groups), out_shape=pltpu.V...  19.8 us
    unnamed x1, local copies, waits for them, and re-layouts  0.71 us

profile of v3, /device:TPU:5, one launch (start us, length us, event | category | flops | bytes accessed | tf_op | source)
XLA Modules:
  0.0 20.5 jit_solution(10832260667946075514)
XLA Ops:
  0.0 19.8 %mixer.1 = bf16[128,1024]{1,0:T(8,128)(2,1)S(1)} custom-call(bf16[128,1024]{1,0:T(8,128)(2,1)} %q_hbm.1, bf16[128,1024]{1,0:T(8,128)(2,1)} %k_hbm.1, bf16[128,1024]{1,0:T(8,128)(2,1)} %v_hbm.1, f32[3,3,1024]{2,1,0:T(4,128)} %fir_hbm.1, f32[1,1024]{1,0:T(1,128)} %bitcast.3, bf16[8,512]{1,0:T(8,128)(2,1)} %taps_hbm.1, s32[1,128]{1,0:T(1,128)} %bitcast.5, ...), custom_call_target="tpu_custom_call" | custom-call | flops 100663296 | bytes 1048576 | tf_op jit(solution)/shard_map/mixer/pallas_call | solution.py:230
  19.8 0.7 %copy.10 = bf16[128,1024]{1,0:T(8,128)(2,1)} copy(bf16[128,1024]{1,0:T(8,128)(2,1)S(1)} %mixer.1) | data formatting | bytes 524288

commit v4 on v3

--- a/solution.py
+++ b/solution.py
@@ -21,14 +21,14 @@
 def kernel(
     n, m, groups,
     q_hbm, k_hbm, v_hbm, fir_hbm, skip_hbm, taps_hbm, seg_hbm, gain_hbm, out,
-    qbuf, kbuf, vbuf, fir, skip, taps, seg, gain, own, slots, aux, fixes, mats, acc, sqs,
-    in_sem, aux_send, aux_recv, kv_send, kv_recv, fwd_send, sq_send, sq_recv,
+    qbuf, kbuf, vbuf, fir, skip, taps, seg, gain, own, slots, halo, edges, mats, acc, sqs,
+    in_sem, halo_sem, edge_send, edge_recv, kv_send, kv_recv, fwd_send, sq_send, sq_recv,
 ):
     me, gi = lax.axis_index("ctx"), lax.axis_index("grp")
     tokens, width = qbuf.shape
     far = n - 2
     relay = n == 4
-    relayed = groups - max(1, groups // 4)
+    relayed = groups - max(1, groups // 8)
     ahead = 2
 
     pairs = (
@@ -43,9 +43,14 @@
         pl.semaphore_signal(barrier, inc=1, device_id={"ctx": lax.rem(me + d, n)}, device_id_type=MESH)
     for e in range(1, m):
         pl.semaphore_signal(barrier, inc=1, device_id={"grp": lax.rem(gi + e, m)}, device_id_type=MESH)
-    def aux_copy(d, peer):
-        return pltpu.make_async_remote_copy(
-            src_ref=aux.at[0], dst_ref=aux.at[d], send_sem=aux_send.at[d - 1], recv_sem=aux_recv.at[d - 1],
+    def halo_copy(peer):
+        return pltpu.make_async_remote_copy(
+            src_ref=halo.at[0], dst_ref=halo.at[1], send_sem=halo_sem.at[0], recv_sem=halo_sem.at[1],
+            device_id={"ctx": peer}, device_id_type=MESH)
+
+    def edge_copy(d, peer):
+        return pltpu.make_async_remote_copy(
+            src_ref=edges.at[0], dst_ref=edges.at[d], send_sem=edge_send.at[d - 1], recv_sem=edge_recv.at[d - 1],
             device_id={"ctx": peer}, device_id_type=MESH)
 
     def kv_copy(d, g, peer):
@@ -75,20 +80,15 @@
     for load in loads:
         load.wait()
 
-    def last8(ref):
-        return ref[tokens - 16 :, :].astype(F32)[8:]
-
-    def first8(ref):
-        return ref[:16, :].astype(F32)[:8]
-
-    seg_f = seg[...].astype(F32)
-    seg_tile = jnp.concatenate([jnp.broadcast_to(seg_f, (8, GW))] * groups, axis=1)
-    upper = jnp.where(
-        row8 < 4,
-        jnp.where(row8 < 2, pltpu.roll(last8(kbuf), 2, 0), pltpu.roll(first8(kbuf), 2, 0)),
-        jnp.where(row8 < 6, pltpu.roll(last8(vbuf), 6, 0), pltpu.roll(first8(vbuf), 6, 0)))
-    lower = jnp.where(row8 < 2, pltpu.roll(last8(qbuf), 2, 0), seg_tile)
-    aux[0] = jnp.concatenate([upper, lower], axis=0).astype(BF16)
+    def last8(ref, by):
+        return pltpu.roll(ref[tokens - 16 :, :].astype(F32)[8:], by, 0)
+
+    def first8(ref, by):
+        return pltpu.roll(ref[:16, :].astype(F32)[:8], by, 0)
+
+    half = width // 2
+    last = jnp.where(row8 < 2, last8(kbuf, 2), jnp.where(row8 < 4, last8(qbuf, 4), last8(vbuf, 6)))
+    halo[0] = jnp.concatenate([last[:, :half], last[:, half:]], axis=0).astype(BF16)
 
     def product(g):
         lane = slice(g * GW, (g + 1) * GW)
@@ -108,36 +108,57 @@
 
     product(0)
     pl.semaphore_wait(barrier, n - 1 + m - 1)
-    for d in range(1, n):
+    @pl.when(me + 1 < n)
+    def _():
+        halo_copy(me + 1).start()
+
+    send_chunk(0)
+    early = min(3, groups)
+    for g in range(1, early):
+        product(g)
+        send_chunk(g)
+
+    @pl.when(me >= 1)
+    def _():
+        halo_copy(me - 1).wait_recv()
+
+    before = halo[1].astype(F32)
+    before = jnp.where(me >= 1, jnp.concatenate([before[:8], before[8:]], axis=1), 0.0)
+    edge = jnp.where(
+        lax.rem(row8, 4) < 2, before, jnp.where(row8 < 4, first8(kbuf, 2), first8(vbuf, 6)))
+    tap = [jnp.where(row8 < 4, fir[1, i : i + 1, :], fir[2, i : i + 1, :]) for i in range(3)]
+    both = tap[0] * edge + tap[1] * pltpu.roll(edge, 1, 0) + tap[2] * pltpu.roll(edge, 2, 0)
+    fix = pltpu.roll(both * pltpu.roll(both, 4, 0), 6, 0)
+    small8 = row8[:, :GW]
+    folded = [jnp.zeros((8, GW), F32)] * 2
+    for g in range(groups):
+        t, j = g // 4, 2 * (g % 4)
+        piece = fix[:, g * GW : (g + 1) * GW]
+        piece = pltpu.roll(piece, j, 0) if j else piece
+        folded[t] = jnp.where((small8 >= j) & (small8 < j + 2), piece, folded[t])
+    seg_f = seg[...].astype(F32)
+    edges[0] = jnp.concatenate(
+        [jnp.concatenate(folded, axis=0), jnp.broadcast_to(seg_f, (16, GW))], axis=1).astype(BF16)
+    for d in range(1, far + 1):
         @pl.when(me + d < n)
         def _():
-            aux_copy(d, me + d).start()
-    send_chunk(0)
-    for g in range(1, groups):
+            edge_copy(d, me + d).start()
+    for g in range(early, groups):
         product(g)
         send_chunk(g)
-
-    for d in range(1, n):
+    for d in range(1, far + 1):
         @pl.when(me >= d)
         def _():
-            aux_copy(d, me - d).wait_recv()
-
-    for d in range(far + 1):
-        @pl.when(me - d >= 1)
-        def _():
-            before, after = aux[d + 1].astype(F32)[:8], aux[d].astype(F32)[:8]
-            edge = jnp.where(lax.rem(row8, 4) < 2, before, after)
-            tap = [jnp.where(row8 < 4, fir[1, i : i + 1, :], fir[2, i : i + 1, :]) for i in range(3)]
-            both = tap[0] * edge + tap[1] * pltpu.roll(edge, 1, 0) + tap[2] * pltpu.roll(edge, 2, 0)
-            fixes[d] = pltpu.roll(both * pltpu.roll(both, 4, 0), 6, 0)
+            edge_copy(d, me - d).wait_recv()
 
     def block_of(ref, d, g):
-        lane = slice(g * GW, (g + 1) * GW)
+        t, j = g // 4, 2 * (g % 4)
+        first = edges[d].astype(F32)[8 * t : 8 * t + 8, :GW]
+        first = pltpu.roll(first, 8 - j, 0) if j else first
         whole = ref[...]
         top = whole[:16].astype(F32)
-        limit = jnp.where(me - d >= 1, 2, 0)
-        head = jnp.where(row8[:, :GW] < limit, fixes[d, :, lane], top[:8])
-        return jnp.concatenate([jnp.concatenate([head, top[8:]], axis=0).astype(BF16), whole[16:]], axis=0)
+        head = jnp.concatenate([jnp.where(small8 < 2, first, top[:8]), top[8:]], axis=0)
+        return jnp.concatenate([head.astype(BF16), whole[16:]], axis=0)
 
     flip = (rows + cols == GW - 1).astype(BF16)
     target = jnp.broadcast_to(seg_f, (tokens, GW)).T
@@ -149,7 +170,7 @@
         nearer = 0.0
         for d in range(far + 1):
             turned = pltpu.roll(jnp.broadcast_to(back[d][g : g + 1], (tokens, GW)), 1, 1, stride=1, stride_axis=0)
-            same = aux[d].astype(F32)[10:11, :GW] == target
+            same = edges[d].astype(F32)[:1, GW:] == target
             mats[d] = jnp.where(same, jnp.where(cols <= rows, turned, nearer), 0.0).astype(BF16)
             nearer = turned
 
@@ -163,9 +184,8 @@
         block = block_of(own.at[g], 0, g)
         acc[g] = jnp.dot(mats[0], block, preferred_element_type=F32) + skip[:, lane] * block.astype(F32)
         x = qbuf[:, lane].astype(F32)
-        halo = jnp.where(me >= 1, aux[1, :, lane].astype(F32), 0.0)
-        one = jnp.where(rows < 1, halo[9:10], pltpu.roll(x, 1, 0))
-        two = jnp.where(rows < 1, halo[8:9], jnp.where(rows < 2, halo[9:10], pltpu.roll(x, 2, 0)))
+        one = jnp.where(rows < 1, before[3:4, lane], pltpu.roll(x, 1, 0))
+        two = jnp.where(rows < 1, before[2:3, lane], jnp.where(rows < 2, before[3:4, lane], pltpu.roll(x, 2, 0)))
         query = fir[0, 0:1, lane] * x + fir[0, 1:2, lane] * one + fir[0, 2:3, lane] * two
         for d in range(far, 0, -1):
             @pl.when(me >= d)
@@ -203,10 +223,14 @@
 
     for e in range(1, m):
         sq_copy(e, lax.rem(gi + e, m)).wait_send()
-    for d in range(1, n):
+    @pl.when(me + 1 < n)
+    def _():
+        halo_copy(me + 1).wait_send()
+
+    for d in range(1, far + 1):
         @pl.when(me + d < n)
         def _():
-            aux_copy(d, me + d).wait_send()
+            edge_copy(d, me + d).wait_send()
     for d in range(1, far + 1):
         for g in range(groups):
             @pl.when(sends(d, g))
@@ -243,14 +267,15 @@
             pltpu.VMEM((1, width), F32),
             pltpu.VMEM(block, BF16),
             pltpu.VMEM((far,) + block, BF16),
-            pltpu.VMEM((n, 16, width), BF16),
-            pltpu.VMEM((far + 1, 8, width), F32),
+            pltpu.VMEM((2, 16, width // 2), BF16),
+            pltpu.VMEM((far + 1, 16, 2 * GW), BF16),
             pltpu.VMEM((far + 1, tokens, GW), BF16),
             pltpu.VMEM(block, F32),
             pltpu.VMEM((m, 8, tokens), F32),
             dma((8,)),
-            dma((n - 1,)),
-            dma((n - 1,)),
+            dma((2,)),
+            dma((far,)),
+            dma((far,)),
             dma((far, groups)),
             dma((far, groups)),
             dma((groups,)),

time: 20.7 us -> 21.5 us (1.039)
  Pallas kernels: 19.8 us -> 20.6 us
    pallas_call x1, Pallas kernels: 19.8 us -> 20.6 us  [on_device(): pl.pallas_call(functools.partial(kernel, n, m, groups), out_shape=pltpu.V...]
where the time goes in v4:
time: 21.5 us; the launch traced here: 21.3 us
  Pallas kernels  20.6 us (96%)
  local copies, waits for them, and re-layouts  0.71 us (3%)
    pallas_call x1, Pallas kernels, on_device(): pl.pallas_call(functools.partial(kernel, n, m, groups), out_shape=pltpu.V...  20.6 us
    unnamed x1, local copies, waits for them, and re-layouts  0.71 us

profile of v4, /device:TPU:5, one launch (start us, length us, event | category | flops | bytes accessed | tf_op | source)
XLA Modules:
  0.0 21.3 jit_solution(8021116795228175252)
XLA Ops:
  0.0 20.6 %mixer.1 = bf16[128,1024]{1,0:T(8,128)(2,1)S(1)} custom-call(bf16[128,1024]{1,0:T(8,128)(2,1)} %q_hbm.1, bf16[128,1024]{1,0:T(8,128)(2,1)} %k_hbm.1, bf16[128,1024]{1,0:T(8,128)(2,1)} %v_hbm.1, f32[3,3,1024]{2,1,0:T(4,128)} %fir_hbm.1, f32[1,1024]{1,0:T(1,128)} %bitcast.3, bf16[8,512]{1,0:T(8,128)(2,1)} %taps_hbm.1, s32[1,128]{1,0:T(1,128)} %bitcast.5, ...), custom_call_target="tpu_custom_call" | custom-call | flops 100663296 | bytes 1048576 | tf_op jit(solution)/shard_map/mixer/pallas_call | solution.py:254
  20.6 0.7 %copy.10 = bf16[128,1024]{1,0:T(8,128)(2,1)} copy(bf16[128,1024]{1,0:T(8,128)(2,1)S(1)} %mixer.1) | data formatting | bytes 524288

commit v5 on v4

--- a/solution.py
+++ b/solution.py
@@ -21,7 +21,7 @@
 def kernel(
     n, m, groups,
     q_hbm, k_hbm, v_hbm, fir_hbm, skip_hbm, taps_hbm, seg_hbm, gain_hbm, out,
-    qbuf, kbuf, vbuf, fir, skip, taps, seg, gain, own, slots, halo, edges, mats, acc, sqs,
+    qbuf, kbuf, vbuf, fir, skip, taps, seg, gain, own, slots, halo, edges, mats, masks, acc, fq, sqs,
     in_sem, halo_sem, edge_send, edge_recv, kv_send, kv_recv, fwd_send, sq_send, sq_recv,
 ):
     me, gi = lax.axis_index("ctx"), lax.axis_index("grp")
@@ -29,7 +29,6 @@
     far = n - 2
     relay = n == 4
     relayed = groups - max(1, groups // 8)
-    ahead = 2
 
     pairs = (
         (k_hbm, kbuf), (v_hbm, vbuf), (q_hbm, qbuf), (fir_hbm, fir),
@@ -143,13 +142,13 @@
         @pl.when(me + d < n)
         def _():
             edge_copy(d, me + d).start()
+    passed = 0
     for g in range(early, groups):
         product(g)
         send_chunk(g)
-    for d in range(1, far + 1):
-        @pl.when(me >= d)
-        def _():
-            edge_copy(d, me - d).wait_recv()
+        if g >= early + 2:
+            pass_on(passed)
+            passed += 1
 
     def block_of(ref, d, g):
         t, j = g // 4, 2 * (g % 4)
@@ -162,31 +161,42 @@
 
     flip = (rows + cols == GW - 1).astype(BF16)
     target = jnp.broadcast_to(seg_f, (tokens, GW)).T
+
+    def mask(d):
+        return jnp.where(edges[d].astype(F32)[:1, GW:] == target, 1.0, 0.0).astype(BF16)
+
+    masks[0] = mask(0)
     back = [
         jnp.dot(taps[:, d * GW : (d + 1) * GW], flip, preferred_element_type=F32) for d in range(far + 1)
     ]
-
-    def matrices(g):
+    for g in range(groups):
+        lane = slice(g * GW, (g + 1) * GW)
         nearer = 0.0
         for d in range(far + 1):
             turned = pltpu.roll(jnp.broadcast_to(back[d][g : g + 1], (tokens, GW)), 1, 1, stride=1, stride_axis=0)
-            same = edges[d].astype(F32)[:1, GW:] == target
-            mats[d] = jnp.where(same, jnp.where(cols <= rows, turned, nearer), 0.0).astype(BF16)
+            mats[d, g] = jnp.where(cols <= rows, turned, nearer).astype(BF16)
             nearer = turned
-
-    squares = jnp.zeros((tokens, GW), F32)
-    for g in range(ahead):
-        pass_on(g)
-    for g in range(groups):
-        lane = slice(g * GW, (g + 1) * GW)
-        pass_on(g + ahead)
-        matrices(g)
         block = block_of(own.at[g], 0, g)
-        acc[g] = jnp.dot(mats[0], block, preferred_element_type=F32) + skip[:, lane] * block.astype(F32)
+        acc[g] = (jnp.dot(mats[0, g] * masks[0], block, preferred_element_type=F32)
+                  + skip[:, lane] * block.astype(F32))
         x = qbuf[:, lane].astype(F32)
         one = jnp.where(rows < 1, before[3:4, lane], pltpu.roll(x, 1, 0))
         two = jnp.where(rows < 1, before[2:3, lane], jnp.where(rows < 2, before[3:4, lane], pltpu.roll(x, 2, 0)))
-        query = fir[0, 0:1, lane] * x + fir[0, 1:2, lane] * one + fir[0, 2:3, lane] * two
+        fq[g] = fir[0, 0:1, lane] * x + fir[0, 1:2, lane] * one + fir[0, 2:3, lane] * two
+        if g % 4 == 3:
+            pass_on(passed)
+            passed += 1
+
+    for d in range(1, far + 1):
+        @pl.when(me >= d)
+        def _():
+            edge_copy(d, me - d).wait_recv()
+            masks[d] = mask(d)
+
+    squares = jnp.zeros((tokens, GW), F32)
+    for g in range(groups):
+        pass_on(passed)
+        passed += 1
         for d in range(far, 0, -1):
             @pl.when(me >= d)
             def _():
@@ -196,8 +206,9 @@
                         kv_copy(d, g, me - d).wait_recv()
                 else:
                     kv_copy(d, g, me - d).wait_recv()
-                acc[g] += jnp.dot(mats[d], block_of(slots.at[d - 1, g], d, g), preferred_element_type=F32)
-        gated = query * acc[g]
+                acc[g] += jnp.dot(
+                    mats[d, g] * masks[d], block_of(slots.at[d - 1, g], d, g), preferred_element_type=F32)
+        gated = fq[g] * acc[g]
         acc[g] = gated
         squares += gated * gated
 
@@ -269,7 +280,9 @@
             pltpu.VMEM((far,) + block, BF16),
             pltpu.VMEM((2, 16, width // 2), BF16),
             pltpu.VMEM((far + 1, 16, 2 * GW), BF16),
+            pltpu.VMEM((far + 1,) + block, BF16),
             pltpu.VMEM((far + 1, tokens, GW), BF16),
+            pltpu.VMEM(block, F32),
             pltpu.VMEM(block, F32),
             pltpu.VMEM((m, 8, tokens), F32),
             dma((8,)),

time: 21.5 us -> 19.5 us (0.907)
  Pallas kernels: 20.6 us -> 18.6 us
    pallas_call x1, Pallas kernels: 20.6 us -> 18.6 us  [on_device(): pl.pallas_call(functools.partial(kernel, n, m, groups), out_shape=pltpu.V...]
where the time goes in v5:
time: 19.5 us; the launch traced here: 19.4 us
  Pallas kernels  18.6 us (95%)
  local copies, waits for them, and re-layouts  0.71 us (4%)
    pallas_call x1, Pallas kernels, on_device(): pl.pallas_call(functools.partial(kernel, n, m, groups), out_shape=pltpu.V...  18.6 us
    unnamed x1, local copies, waits for them, and re-layouts  0.71 us

profile of v5, /device:TPU:5, one launch (start us, length us, event | category | flops | bytes accessed | tf_op | source)
XLA Modules:
  0.0 19.4 jit_solution(17337059647815894326)
XLA Ops:
  0.0 18.6 %mixer.1 = bf16[128,1024]{1,0:T(8,128)(2,1)S(1)} custom-call(bf16[128,1024]{1,0:T(8,128)(2,1)} %q_hbm.1, bf16[128,1024]{1,0:T(8,128)(2,1)} %k_hbm.1, bf16[128,1024]{1,0:T(8,128)(2,1)} %v_hbm.1, f32[3,3,1024]{2,1,0:T(4,128)} %fir_hbm.1, f32[1,1024]{1,0:T(1,128)} %bitcast.3, bf16[8,512]{1,0:T(8,128)(2,1)} %taps_hbm.1, s32[1,128]{1,0:T(1,128)} %bitcast.5, ...), custom_call_target="tpu_custom_call" | custom-call | flops 100663296 | bytes 1048576 | tf_op jit(solution)/shard_map/mixer/pallas_call | solution.py:265
  18.7 0.7 %copy.10 = bf16[128,1024]{1,0:T(8,128)(2,1)} copy(bf16[128,1024]{1,0:T(8,128)(2,1)S(1)} %mixer.1) | data formatting | bytes 524288

commit v6 on v5

--- a/solution.py
+++ b/solution.py
@@ -64,7 +64,7 @@
 
     def sends(d, g):
         there = me + d < n
-        return there & (me != 1) if relay and d == 1 and g < relayed else there
+        return there & (me != 1) if relay and d == 1 else there
 
     def pass_on(g):
         if relay and g < relayed:
@@ -100,16 +100,24 @@
         own[g] = (filtered(kbuf, 1) * filtered(vbuf, 2)).astype(BF16)
 
     def send_chunk(g):
-        for d in range(1, far + 1):
+        for d in range(far, 0, -1):
             @pl.when(sends(d, g))
             def _():
                 kv_copy(d, g, me + d).start()
 
-    product(0)
+    direct = range(relayed, groups) if relay else range(0)
+    for g in (*direct, 0):
+        product(g)
     pl.semaphore_wait(barrier, n - 1 + m - 1)
     @pl.when(me + 1 < n)
     def _():
         halo_copy(me + 1).start()
+
+    if relay:
+        @pl.when(me == 1)
+        def _():
+            for g in direct:
+                kv_copy(1, g, 2).start()
 
     send_chunk(0)
     early = min(3, groups)
@@ -144,7 +152,8 @@
             edge_copy(d, me + d).start()
     passed = 0
     for g in range(early, groups):
-        product(g)
+        if g not in direct:
+            product(g)
         send_chunk(g)
         if g >= early + 2:
             pass_on(passed)
@@ -248,6 +257,11 @@
             def _():
                 kv_copy(d, g, me + d).wait_send()
     if relay:
+        @pl.when(me == 1)
+        def _():
+            for g in direct:
+                kv_copy(1, g, 2).wait_send()
+
         @pl.when(me == 3)
         def _():
             for g in range(relayed):

time: 19.5 us -> 19.5 us (level)
  no operation moved by 1% of the time
where the time goes in v6:
time: 19.5 us; the launch traced here: 19.4 us
  Pallas kernels  18.6 us (95%)
  local copies, waits for them, and re-layouts  0.71 us (4%)
    pallas_call x1, Pallas kernels, on_device(): pl.pallas_call(functools.partial(kernel, n, m, groups), out_shape=pltpu.V...  18.6 us
    unnamed x1, local copies, waits for them, and re-layouts  0.71 us

profile of v6, /device:TPU:5, one launch (start us, length us, event | category | flops | bytes accessed | tf_op | source)
XLA Modules:
  0.0 19.4 jit_solution(6330965385177694114)
XLA Ops:
  0.0 18.6 %mixer.1 = bf16[128,1024]{1,0:T(8,128)(2,1)S(1)} custom-call(bf16[128,1024]{1,0:T(8,128)(2,1)} %q_hbm.1, bf16[128,1024]{1,0:T(8,128)(2,1)} %k_hbm.1, bf16[128,1024]{1,0:T(8,128)(2,1)} %v_hbm.1, f32[3,3,1024]{2,1,0:T(4,128)} %fir_hbm.1, f32[1,1024]{1,0:T(1,128)} %bitcast.3, bf16[8,512]{1,0:T(8,128)(2,1)} %taps_hbm.1, s32[1,128]{1,0:T(1,128)} %bitcast.5, ...), custom_call_target="tpu_custom_call" | custom-call | flops 100663296 | bytes 1048576 | tf_op jit(solution)/shard_map/mixer/pallas_call | solution.py:279
  18.7 0.7 %copy.10 = bf16[128,1024]{1,0:T(8,128)(2,1)} copy(bf16[128,1024]{1,0:T(8,128)(2,1)S(1)} %mixer.1) | data formatting | bytes 524288

commit v7 on v6

--- a/solution.py
+++ b/solution.py
@@ -28,7 +28,7 @@
     tokens, width = qbuf.shape
     far = n - 2
     relay = n == 4
-    relayed = groups - max(1, groups // 8)
+    relayed = groups - max(1, groups // 4)
 
     pairs = (
         (k_hbm, kbuf), (v_hbm, vbuf), (q_hbm, qbuf), (fir_hbm, fir),
@@ -192,7 +192,7 @@
         one = jnp.where(rows < 1, before[3:4, lane], pltpu.roll(x, 1, 0))
         two = jnp.where(rows < 1, before[2:3, lane], jnp.where(rows < 2, before[3:4, lane], pltpu.roll(x, 2, 0)))
         fq[g] = fir[0, 0:1, lane] * x + fir[0, 1:2, lane] * one + fir[0, 2:3, lane] * two
-        if g % 4 == 3:
+        if g % 3 == 1:
             pass_on(passed)
             passed += 1
 
@@ -230,19 +230,6 @@
 
     for e in range(1, m):
         sq_copy(e, lax.rem(gi + e, m)).start()
-    for e in range(1, m):
-        sq_copy(e, lax.rem(gi + m - e, m)).wait_recv()
-    total = sqs[0]
-    for e in range(1, m):
-        total += sqs[e]
-    scale = lax.rsqrt(jnp.sum(total, axis=0, keepdims=True) / D + 1e-06)
-    scale = jnp.broadcast_to(scale, (GW, tokens)).T
-    for g in range(groups):
-        lane = slice(g * GW, (g + 1) * GW)
-        out[:, lane] = (acc[g] * scale * gain[:, lane]).astype(BF16)
-
-    for e in range(1, m):
-        sq_copy(e, lax.rem(gi + e, m)).wait_send()
     @pl.when(me + 1 < n)
     def _():
         halo_copy(me + 1).wait_send()
@@ -266,6 +253,20 @@
         def _():
             for g in range(relayed):
                 forward(g).wait_send()
+
+    for e in range(1, m):
+        sq_copy(e, lax.rem(gi + m - e, m)).wait_recv()
+    total = sqs[0]
+    for e in range(1, m):
+        total += sqs[e]
+    scale = lax.rsqrt(jnp.sum(total, axis=0, keepdims=True) / D + 1e-06)
+    scale = jnp.broadcast_to(scale, (GW, tokens)).T
+    for g in range(groups):
+        lane = slice(g * GW, (g + 1) * GW)
+        out[:, lane] = (acc[g] * scale * gain[:, lane]).astype(BF16)
+
+    for e in range(1, m):
+        sq_copy(e, lax.rem(gi + e, m)).wait_send()
 
 
 def on_device(n, m, q_in, k_in, v_in, fir, skip, taps, segments, gain):

time: 19.5 us -> 19.4 us (level)
  no operation moved by 1% of the time
where the time goes in v7:
time: 19.4 us; the launch traced here: 19.3 us
  Pallas kernels  18.6 us (96%)
  local copies, waits for them, and re-layouts  0.71 us (4%)
    pallas_call x1, Pallas kernels, on_device(): pl.pallas_call(functools.partial(kernel, n, m, groups), out_shape=pltpu.V...  18.6 us
    unnamed x1, local copies, waits for them, and re-layouts  0.71 us

profile of v7, /device:TPU:5, one launch (start us, length us, event | category | flops | bytes accessed | tf_op | source)
XLA Modules:
  0.0 19.3 jit_solution(8506533197996676919)
XLA Ops:
  0.0 18.6 %mixer.1 = bf16[128,1024]{1,0:T(8,128)(2,1)S(1)} custom-call(bf16[128,1024]{1,0:T(8,128)(2,1)} %q_hbm.1, bf16[128,1024]{1,0:T(8,128)(2,1)} %k_hbm.1, bf16[128,1024]{1,0:T(8,128)(2,1)} %v_hbm.1, f32[3,3,1024]{2,1,0:T(4,128)} %fir_hbm.1, f32[1,1024]{1,0:T(1,128)} %bitcast.3, bf16[8,512]{1,0:T(8,128)(2,1)} %taps_hbm.1, s32[1,128]{1,0:T(1,128)} %bitcast.5, ...), custom_call_target="tpu_custom_call" | custom-call | flops 100663296 | bytes 1048576 | tf_op jit(solution)/shard_map/mixer/pallas_call | solution.py:280
  18.6 0.7 %copy.10 = bf16[128,1024]{1,0:T(8,128)(2,1)} copy(bf16[128,1024]{1,0:T(8,128)(2,1)S(1)} %mixer.1) | data formatting | bytes 524288

commit v8 on v7

--- a/solution.py
+++ b/solution.py
@@ -18,17 +18,29 @@
     return jnp.where(rows >= by, pltpu.roll(x, by, 0), 0.0)
 
 
+def each(start, stop, step):
+    def body(g, carry):
+        step(g)
+        return carry
+
+    lax.fori_loop(start, stop, body, 0)
+
+
+def lanes(g):
+    return pl.ds(pl.multiple_of(g * GW, GW), GW)
+
+
 def kernel(
     n, m, groups,
     q_hbm, k_hbm, v_hbm, fir_hbm, skip_hbm, taps_hbm, seg_hbm, gain_hbm, out,
-    qbuf, kbuf, vbuf, fir, skip, taps, seg, gain, own, slots, halo, edges, mats, masks, acc, fq, sqs,
+    qbuf, kbuf, vbuf, fir, skip, taps, seg, gain, own, slots, halo, edges, fixes, before, backs, mats, masks, acc, fq, sqs,
     in_sem, halo_sem, edge_send, edge_recv, kv_send, kv_recv, fwd_send, sq_send, sq_recv,
 ):
     me, gi = lax.axis_index("ctx"), lax.axis_index("grp")
     tokens, width = qbuf.shape
     far = n - 2
     relay = n == 4
-    relayed = groups - max(1, groups // 4)
+    relayed = groups - max(1, groups // 4) if relay else groups
 
     pairs = (
         (k_hbm, kbuf), (v_hbm, vbuf), (q_hbm, qbuf), (fir_hbm, fir),
@@ -62,13 +74,13 @@
             src_ref=slots.at[1, g], dst_ref=slots.at[0, g], send_sem=fwd_send.at[g],
             recv_sem=kv_recv.at[0, g], device_id={"ctx": 2}, device_id_type=MESH)
 
-    def sends(d, g):
+    def sends(d):
         there = me + d < n
         return there & (me != 1) if relay and d == 1 else there
 
     def pass_on(g):
-        if relay and g < relayed:
-            @pl.when(me == 3)
+        if relay:
+            @pl.when((me == 3) & (g < relayed))
             def _():
                 kv_copy(2, g, 1).wait_recv()
                 forward(g).start()
@@ -90,7 +102,7 @@
     halo[0] = jnp.concatenate([last[:, :half], last[:, half:]], axis=0).astype(BF16)
 
     def product(g):
-        lane = slice(g * GW, (g + 1) * GW)
+        lane = lanes(g)
 
         def filtered(ref, a):
             x = ref[:, lane].astype(F32)
@@ -101,13 +113,11 @@
 
     def send_chunk(g):
         for d in range(far, 0, -1):
-            @pl.when(sends(d, g))
+            @pl.when(sends(d))
             def _():
                 kv_copy(d, g, me + d).start()
 
-    direct = range(relayed, groups) if relay else range(0)
-    for g in (*direct, 0):
-        product(g)
+    each(0, groups - relayed + 1, lambda i: product(lax.rem(i + relayed, groups)))
     pl.semaphore_wait(barrier, n - 1 + m - 1)
     @pl.when(me + 1 < n)
     def _():
@@ -116,23 +126,30 @@
     if relay:
         @pl.when(me == 1)
         def _():
-            for g in direct:
+            for g in range(relayed, groups):
                 kv_copy(1, g, 2).start()
 
     send_chunk(0)
     early = min(3, groups)
-    for g in range(1, early):
-        product(g)
+
+    def made_and_sent(g):
+        @pl.when(g < relayed)
+        def _():
+            product(g)
+
         send_chunk(g)
+
+    each(1, early, made_and_sent)
 
     @pl.when(me >= 1)
     def _():
         halo_copy(me - 1).wait_recv()
 
-    before = halo[1].astype(F32)
-    before = jnp.where(me >= 1, jnp.concatenate([before[:8], before[8:]], axis=1), 0.0)
+    came = halo[1].astype(F32)
+    came = jnp.where(me >= 1, jnp.concatenate([came[:8], came[8:]], axis=1), 0.0)
+    before[...] = came
     edge = jnp.where(
-        lax.rem(row8, 4) < 2, before, jnp.where(row8 < 4, first8(kbuf, 2), first8(vbuf, 6)))
+        lax.rem(row8, 4) < 2, came, jnp.where(row8 < 4, first8(kbuf, 2), first8(vbuf, 6)))
     tap = [jnp.where(row8 < 4, fir[1, i : i + 1, :], fir[2, i : i + 1, :]) for i in range(3)]
     both = tap[0] * edge + tap[1] * pltpu.roll(edge, 1, 0) + tap[2] * pltpu.roll(edge, 2, 0)
     fix = pltpu.roll(both * pltpu.roll(both, 4, 0), 6, 0)
@@ -141,6 +158,7 @@
     for g in range(groups):
         t, j = g // 4, 2 * (g % 4)
         piece = fix[:, g * GW : (g + 1) * GW]
+        fixes[0, g] = piece
         piece = pltpu.roll(piece, j, 0) if j else piece
         folded[t] = jnp.where((small8 >= j) & (small8 < j + 2), piece, folded[t])
     seg_f = seg[...].astype(F32)
@@ -150,19 +168,20 @@
         @pl.when(me + d < n)
         def _():
             edge_copy(d, me + d).start()
-    passed = 0
-    for g in range(early, groups):
-        if g not in direct:
-            product(g)
-        send_chunk(g)
-        if g >= early + 2:
-            pass_on(passed)
-            passed += 1
+    passed = early + 2
+
+    def late(g):
+        made_and_sent(g)
+
+        @pl.when(g >= passed)
+        def _():
+            pass_on(g - passed)
+
+    each(early, groups, late)
+    passed = max(0, groups - passed)
 
     def block_of(ref, d, g):
-        t, j = g // 4, 2 * (g % 4)
-        first = edges[d].astype(F32)[8 * t : 8 * t + 8, :GW]
-        first = pltpu.roll(first, 8 - j, 0) if j else first
+        first = fixes[d, g]
         whole = ref[...]
         top = whole[:16].astype(F32)
         head = jnp.concatenate([jnp.where(small8 < 2, first, top[:8]), top[8:]], axis=0)
@@ -175,42 +194,52 @@
         return jnp.where(edges[d].astype(F32)[:1, GW:] == target, 1.0, 0.0).astype(BF16)
 
     masks[0] = mask(0)
-    back = [
-        jnp.dot(taps[:, d * GW : (d + 1) * GW], flip, preferred_element_type=F32) for d in range(far + 1)
-    ]
-    for g in range(groups):
-        lane = slice(g * GW, (g + 1) * GW)
+    for d in range(far + 1):
+        backs[d] = jnp.dot(taps[:, d * GW : (d + 1) * GW], flip, preferred_element_type=F32)
+
+    def prepare(g):
+        lane = lanes(g)
         nearer = 0.0
         for d in range(far + 1):
-            turned = pltpu.roll(jnp.broadcast_to(back[d][g : g + 1], (tokens, GW)), 1, 1, stride=1, stride_axis=0)
+            back = jnp.broadcast_to(backs[d, pl.ds(g, 1), :], (tokens, GW))
+            turned = pltpu.roll(back, 1, 1, stride=1, stride_axis=0)
             mats[d, g] = jnp.where(cols <= rows, turned, nearer).astype(BF16)
             nearer = turned
         block = block_of(own.at[g], 0, g)
         acc[g] = (jnp.dot(mats[0, g] * masks[0], block, preferred_element_type=F32)
                   + skip[:, lane] * block.astype(F32))
         x = qbuf[:, lane].astype(F32)
-        one = jnp.where(rows < 1, before[3:4, lane], pltpu.roll(x, 1, 0))
-        two = jnp.where(rows < 1, before[2:3, lane], jnp.where(rows < 2, before[3:4, lane], pltpu.roll(x, 2, 0)))
+        last2, last1 = before[2:3, lane], before[3:4, lane]
+        one = jnp.where(rows < 1, last1, pltpu.roll(x, 1, 0))
+        two = jnp.where(rows < 1, last2, jnp.where(rows < 2, last1, pltpu.roll(x, 2, 0)))
         fq[g] = fir[0, 0:1, lane] * x + fir[0, 1:2, lane] * one + fir[0, 2:3, lane] * two
-        if g % 3 == 1:
-            pass_on(passed)
-            passed += 1
+
+        @pl.when(lax.rem(g, 3) == 1)
+        def _():
+            pass_on(passed + g // 3)
+
+    each(0, groups, prepare)
+    done = passed + (groups + 1) // 3
 
     for d in range(1, far + 1):
         @pl.when(me >= d)
         def _():
             edge_copy(d, me - d).wait_recv()
             masks[d] = mask(d)
-
-    squares = jnp.zeros((tokens, GW), F32)
-    for g in range(groups):
-        pass_on(passed)
-        passed += 1
+            found = edges[d].astype(F32)
+            for g in range(groups):
+                t, j = g // 4, 2 * (g % 4)
+                first = found[8 * t : 8 * t + 8, :GW]
+                fixes[d, g] = pltpu.roll(first, 8 - j, 0) if j else first
+
+    def receive(g, squares):
+        if done < relayed:
+            pass_on(done + g)
         for d in range(far, 0, -1):
             @pl.when(me >= d)
             def _():
-                if relay and d == 2 and g < relayed:
-                    @pl.when(me == 2)
+                if relay and d == 2:
+                    @pl.when((me == 2) | (g >= relayed))
                     def _():
                         kv_copy(d, g, me - d).wait_recv()
                 else:
@@ -219,8 +248,9 @@
                     mats[d, g] * masks[d], block_of(slots.at[d - 1, g], d, g), preferred_element_type=F32)
         gated = fq[g] * acc[g]
         acc[g] = gated
-        squares += gated * gated
-
+        return squares + gated * gated
+
+    squares = lax.fori_loop(0, groups, receive, jnp.zeros((tokens, GW), F32))
     sqs[0] = jnp.sum(squares.T.reshape(GW // 8, 8, tokens), axis=0)
 
     def sq_copy(e, peer):
@@ -230,6 +260,7 @@
 
     for e in range(1, m):
         sq_copy(e, lax.rem(gi + e, m)).start()
+
     @pl.when(me + 1 < n)
     def _():
         halo_copy(me + 1).wait_send()
@@ -240,13 +271,13 @@
             edge_copy(d, me + d).wait_send()
     for d in range(1, far + 1):
         for g in range(groups):
-            @pl.when(sends(d, g))
+            @pl.when(sends(d))
             def _():
                 kv_copy(d, g, me + d).wait_send()
     if relay:
         @pl.when(me == 1)
         def _():
-            for g in direct:
+            for g in range(relayed, groups):
                 kv_copy(1, g, 2).wait_send()
 
         @pl.when(me == 3)
@@ -261,9 +292,12 @@
         total += sqs[e]
     scale = lax.rsqrt(jnp.sum(total, axis=0, keepdims=True) / D + 1e-06)
     scale = jnp.broadcast_to(scale, (GW, tokens)).T
-    for g in range(groups):
-        lane = slice(g * GW, (g + 1) * GW)
+
+    def finish(g):
+        lane = lanes(g)
         out[:, lane] = (acc[g] * scale * gain[:, lane]).astype(BF16)
+
+    each(0, groups, finish)
 
     for e in range(1, m):
         sq_copy(e, lax.rem(gi + e, m)).wait_send()
@@ -295,6 +329,9 @@
             pltpu.VMEM((far,) + block, BF16),
             pltpu.VMEM((2, 16, width // 2), BF16),
             pltpu.VMEM((far + 1, 16, 2 * GW), BF16),
+            pltpu.VMEM((far + 1, groups, 8, GW), F32),
+            pltpu.VMEM((8, width), F32),
+            pltpu.VMEM((far + 1, groups, GW), F32),
             pltpu.VMEM((far + 1,) + block, BF16),
             pltpu.VMEM((far + 1, tokens, GW), BF16),
             pltpu.VMEM(block, F32),

time: 19.4 us -> 20.1 us (1.036)
  Pallas kernels: 18.6 us -> 19.3 us
    pallas_call x1, Pallas kernels: 18.6 us -> 19.3 us  [on_device(): pl.pallas_call(functools.partial(kernel, n, m, groups), out_shape=pltpu.V...]
where the time goes in v8:
time: 20.1 us; the launch traced here: 20 us
  Pallas kernels  19.3 us (96%)
  local copies, waits for them, and re-layouts  0.71 us (4%)
    pallas_call x1, Pallas kernels, on_device(): pl.pallas_call(functools.partial(kernel, n, m, groups), out_shape=pltpu.V...  19.3 us
    unnamed x1, local copies, waits for them, and re-layouts  0.71 us

profile of v8, /device:TPU:5, one launch (start us, length us, event | category | flops | bytes accessed | tf_op | source)
XLA Modules:
  0.0 20.0 jit_solution(13785898429392250585)
XLA Ops:
  0.0 19.3 %mixer.1 = bf16[128,1024]{1,0:T(8,128)(2,1)S(1)} custom-call(bf16[128,1024]{1,0:T(8,128)(2,1)} %q_hbm.1, bf16[128,1024]{1,0:T(8,128)(2,1)} %k_hbm.1, bf16[128,1024]{1,0:T(8,128)(2,1)} %v_hbm.1, f32[3,3,1024]{2,1,0:T(4,128)} %fir_hbm.1, f32[1,1024]{1,0:T(1,128)} %bitcast.3, bf16[8,512]{1,0:T(8,128)(2,1)} %taps_hbm.1, s32[1,128]{1,0:T(1,128)} %bitcast.5, ...), custom_call_target="tpu_custom_call" | custom-call | flops 100663296 | bytes 1048576 | tf_op jit(solution)/shard_map/mixer/pallas_call | solution.py:314
  19.3 0.7 %copy.10 = bf16[128,1024]{1,0:T(8,128)(2,1)} copy(bf16[128,1024]{1,0:T(8,128)(2,1)S(1)} %mixer.1) | data formatting | bytes 524288

commit v9 on v7

--- a/solution.py
+++ b/solution.py
@@ -202,26 +202,50 @@
             edge_copy(d, me - d).wait_recv()
             masks[d] = mask(d)
 
+    def receive(d, g):
+        if relay and d == 2 and g < relayed:
+            @pl.when(me == 2)
+            def _():
+                kv_copy(d, g, me - d).wait_recv()
+        else:
+            kv_copy(d, g, me - d).wait_recv()
+
+    def add_blocks(pair, sources):
+        for g in pair:
+            for d in sources:
+                receive(d, g)
+        for g in pair:
+            left = jnp.concatenate([mats[d, g] * masks[d] for d in sources], axis=1)
+            right = jnp.concatenate([block_of(slots.at[d - 1, g], d, g) for d in sources], axis=0)
+            acc[g] += jnp.dot(left, right, preferred_element_type=F32)
+
     squares = jnp.zeros((tokens, GW), F32)
-    for g in range(groups):
-        pass_on(passed)
-        passed += 1
-        for d in range(far, 0, -1):
-            @pl.when(me >= d)
-            def _():
-                if relay and d == 2 and g < relayed:
-                    @pl.when(me == 2)
-                    def _():
-                        kv_copy(d, g, me - d).wait_recv()
-                else:
-                    kv_copy(d, g, me - d).wait_recv()
-                acc[g] += jnp.dot(
-                    mats[d, g] * masks[d], block_of(slots.at[d - 1, g], d, g), preferred_element_type=F32)
-        gated = fq[g] * acc[g]
-        acc[g] = gated
-        squares += gated * gated
-
-    sqs[0] = jnp.sum(squares.T.reshape(GW // 8, 8, tokens), axis=0)
+    for start in range(0, groups, 2):
+        pair = range(start, min(start + 2, groups))
+        for g in pair:
+            pass_on(passed)
+            passed += 1
+        if relay:
+            pl.when(me == 1)(functools.partial(add_blocks, pair, (1,)))
+            pl.when(me >= 2)(functools.partial(add_blocks, pair, (2, 1)))
+        else:
+            for d in range(far, 0, -1):
+                pl.when(me >= d)(functools.partial(add_blocks, pair, (d,)))
+        for g in pair:
+            gated = fq[g] * acc[g]
+            acc[g] = gated
+            squares += gated * gated
+
+    sqs[0] = jnp.sum(squares.T, axis=0, keepdims=True)
+
+    if m == 8:
+        z, core = lax.div(gi, 2), lax.rem(gi, 2)
+        chips = (3 - z, lax.rem(z + 2, 4), z + 1 - 2 * lax.rem(z, 2))
+        peers = [2 * chip + c for chip in chips for c in (core, 1 - core)] + [2 * z + 1 - core]
+        sources = peers
+    else:
+        peers = [lax.rem(gi + e, m) for e in range(1, m)]
+        sources = [lax.rem(gi + m - e, m) for e in range(1, m)]
 
     def sq_copy(e, peer):
         return pltpu.make_async_remote_copy(
@@ -229,7 +253,8 @@
             device_id={"grp": peer}, device_id_type=MESH)
 
     for e in range(1, m):
-        sq_copy(e, lax.rem(gi + e, m)).start()
+        sq_copy(e, peers[e - 1]).start()
+
     @pl.when(me + 1 < n)
     def _():
         halo_copy(me + 1).wait_send()
@@ -255,18 +280,18 @@
                 forward(g).wait_send()
 
     for e in range(1, m):
-        sq_copy(e, lax.rem(gi + m - e, m)).wait_recv()
+        sq_copy(e, sources[e - 1]).wait_recv()
     total = sqs[0]
     for e in range(1, m):
         total += sqs[e]
-    scale = lax.rsqrt(jnp.sum(total, axis=0, keepdims=True) / D + 1e-06)
+    scale = lax.rsqrt(total / D + 1e-06)
     scale = jnp.broadcast_to(scale, (GW, tokens)).T
     for g in range(groups):
         lane = slice(g * GW, (g + 1) * GW)
         out[:, lane] = (acc[g] * scale * gain[:, lane]).astype(BF16)
 
     for e in range(1, m):
-        sq_copy(e, lax.rem(gi + e, m)).wait_send()
+        sq_copy(e, peers[e - 1]).wait_send()
 
 
 def on_device(n, m, q_in, k_in, v_in, fir, skip, taps, segments, gain):
@@ -299,7 +324,7 @@
             pltpu.VMEM((far + 1, tokens, GW), BF16),
             pltpu.VMEM(block, F32),
             pltpu.VMEM(block, F32),
-            pltpu.VMEM((m, 8, tokens), F32),
+            pltpu.VMEM((m, 1, tokens), F32),
             dma((8,)),
             dma((2,)),
             dma((far,)),

time: 19.4 us -> 18.7 us (0.964)
  Pallas kernels: 18.6 us -> 17.9 us
    pallas_call x1, Pallas kernels: 18.6 us -> 17.9 us  [on_device(): pl.pallas_call(functools.partial(kernel, n, m, groups), out_shape=pltpu.V...]
where the time goes in v9:
time: 18.7 us; the launch traced here: 18.6 us
  Pallas kernels  17.9 us (96%)
  local copies, waits for them, and re-layouts  0.71 us (4%)
    pallas_call x1, Pallas kernels, on_device(): pl.pallas_call(functools.partial(kernel, n, m, groups), out_shape=pltpu.V...  17.9 us
    unnamed x1, local copies, waits for them, and re-layouts  0.71 us

profile of v9, /device:TPU:5, one launch (start us, length us, event | category | flops | bytes accessed | tf_op | source)
XLA Modules:
  0.0 18.6 jit_solution(2164208711389624637)
XLA Ops:
  0.0 17.9 %mixer.1 = bf16[128,1024]{1,0:T(8,128)(2,1)S(1)} custom-call(bf16[128,1024]{1,0:T(8,128)(2,1)} %q_hbm.1, bf16[128,1024]{1,0:T(8,128)(2,1)} %k_hbm.1, bf16[128,1024]{1,0:T(8,128)(2,1)} %v_hbm.1, f32[3,3,1024]{2,1,0:T(4,128)} %fir_hbm.1, f32[1,1024]{1,0:T(1,128)} %bitcast.3, bf16[8,512]{1,0:T(8,128)(2,1)} %taps_hbm.1, s32[1,128]{1,0:T(1,128)} %bitcast.5, ...), custom_call_target="tpu_custom_call" | custom-call | flops 100663296 | bytes 1048576 | tf_op jit(solution)/shard_map/mixer/pallas_call | solution.py:305
  17.9 0.7 %copy.10 = bf16[128,1024]{1,0:T(8,128)(2,1)} copy(bf16[128,1024]{1,0:T(8,128)(2,1)S(1)} %mixer.1) | data formatting | bytes 524288

commit v10 on v9

--- a/solution.py
+++ b/solution.py
@@ -28,7 +28,7 @@
     tokens, width = qbuf.shape
     far = n - 2
     relay = n == 4
-    relayed = groups - max(1, groups // 4)
+    relayed = groups - max(1, groups // 8)
 
     pairs = (
         (k_hbm, kbuf), (v_hbm, vbuf), (q_hbm, qbuf), (fir_hbm, fir),

time: 18.7 us -> 18.9 us (1.011)
  no operation moved by 1% of the time
where the time goes in v10:
time: 18.9 us; the launch traced here: 18.7 us
  Pallas kernels  18 us (95%)
  local copies, waits for them, and re-layouts  0.71 us (4%)
    pallas_call x1, Pallas kernels, on_device(): pl.pallas_call(functools.partial(kernel, n, m, groups), out_shape=pltpu.V...  18 us
    unnamed x1, local copies, waits for them, and re-layouts  0.71 us

profile of v10, /device:TPU:5, one launch (start us, length us, event | category | flops | bytes accessed | tf_op | source)
XLA Modules:
  0.0 18.7 jit_solution(9314692142914070691)
XLA Ops:
  0.0 18.0 %mixer.1 = bf16[128,1024]{1,0:T(8,128)(2,1)S(1)} custom-call(bf16[128,1024]{1,0:T(8,128)(2,1)} %q_hbm.1, bf16[128,1024]{1,0:T(8,128)(2,1)} %k_hbm.1, bf16[128,1024]{1,0:T(8,128)(2,1)} %v_hbm.1, f32[3,3,1024]{2,1,0:T(4,128)} %fir_hbm.1, f32[1,1024]{1,0:T(1,128)} %bitcast.3, bf16[8,512]{1,0:T(8,128)(2,1)} %taps_hbm.1, s32[1,128]{1,0:T(1,128)} %bitcast.5, ...), custom_call_target="tpu_custom_call" | custom-call | flops 100663296 | bytes 1048576 | tf_op jit(solution)/shard_map/mixer/pallas_call | solution.py:305
  18.0 0.7 %copy.10 = bf16[128,1024]{1,0:T(8,128)(2,1)} copy(bf16[128,1024]{1,0:T(8,128)(2,1)S(1)} %mixer.1) | data formatting | bytes 524288

commit v11 on v9

--- a/solution.py
+++ b/solution.py
@@ -101,9 +101,18 @@
 
     def send_chunk(g):
         for d in range(far, 0, -1):
-            @pl.when(sends(d, g))
+            @pl.when(sends(d, g) & (me != 0) if relay and d == 1 else sends(d, g))
             def _():
                 kv_copy(d, g, me + d).start()
+        if relay and g >= lag:
+            late_chunk(g - lag)
+
+    lag = min(2, groups)
+
+    def late_chunk(g):
+        @pl.when(me == 0)
+        def _():
+            kv_copy(1, g, 1).start()
 
     direct = range(relayed, groups) if relay else range(0)
     for g in (*direct, 0):
@@ -155,6 +164,9 @@
         if g not in direct:
             product(g)
         send_chunk(g)
+        if relay and g == groups - 1:
+            for h in range(groups - lag, groups):
+                late_chunk(h)
         if g >= early + 2:
             pass_on(passed)
             passed += 1

time: 18.7 us -> 18.7 us (level)
  no operation moved by 1% of the time
where the time goes in v11:
time: 18.7 us; the launch traced here: 18.6 us
  Pallas kernels  17.9 us (96%)
  local copies, waits for them, and re-layouts  0.71 us (4%)
    pallas_call x1, Pallas kernels, on_device(): pl.pallas_call(functools.partial(kernel, n, m, groups), out_shape=pltpu.V...  17.9 us
    unnamed x1, local copies, waits for them, and re-layouts  0.71 us

profile of v11, /device:TPU:5, one launch (start us, length us, event | category | flops | bytes accessed | tf_op | source)
XLA Modules:
  0.0 18.6 jit_solution(17790861962835920183)
XLA Ops:
  0.0 17.9 %mixer.1 = bf16[128,1024]{1,0:T(8,128)(2,1)S(1)} custom-call(bf16[128,1024]{1,0:T(8,128)(2,1)} %q_hbm.1, bf16[128,1024]{1,0:T(8,128)(2,1)} %k_hbm.1, bf16[128,1024]{1,0:T(8,128)(2,1)} %v_hbm.1, f32[3,3,1024]{2,1,0:T(4,128)} %fir_hbm.1, f32[1,1024]{1,0:T(1,128)} %bitcast.3, bf16[8,512]{1,0:T(8,128)(2,1)} %taps_hbm.1, s32[1,128]{1,0:T(1,128)} %bitcast.5, ...), custom_call_target="tpu_custom_call" | custom-call | flops 100663296 | bytes 1048576 | tf_op jit(solution)/shard_map/mixer/pallas_call | solution.py:317
  17.9 0.7 %copy.10 = bf16[128,1024]{1,0:T(8,128)(2,1)} copy(bf16[128,1024]{1,0:T(8,128)(2,1)S(1)} %mixer.1) | data formatting | bytes 524288

commit v12 on v10

--- a/solution.py
+++ b/solution.py
@@ -192,7 +192,7 @@
         one = jnp.where(rows < 1, before[3:4, lane], pltpu.roll(x, 1, 0))
         two = jnp.where(rows < 1, before[2:3, lane], jnp.where(rows < 2, before[3:4, lane], pltpu.roll(x, 2, 0)))
         fq[g] = fir[0, 0:1, lane] * x + fir[0, 1:2, lane] * one + fir[0, 2:3, lane] * two
-        if g % 3 == 1:
+        if g % 2 == 1:
             pass_on(passed)
             passed += 1
 

time: 18.9 us -> 18.9 us (level)
  no operation moved by 1% of the time
where the time goes in v12:
time: 18.9 us; the launch traced here: 18.7 us
  Pallas kernels  18 us (95%)
  local copies, waits for them, and re-layouts  0.71 us (4%)
    pallas_call x1, Pallas kernels, on_device(): pl.pallas_call(functools.partial(kernel, n, m, groups), out_shape=pltpu.V...  18 us
    unnamed x1, local copies, waits for them, and re-layouts  0.71 us

profile of v12, /device:TPU:5, one launch (start us, length us, event | category | flops | bytes accessed | tf_op | source)
XLA Modules:
  0.0 18.7 jit_solution(748433546199613645)
XLA Ops:
  0.0 18.0 %mixer.1 = bf16[128,1024]{1,0:T(8,128)(2,1)S(1)} custom-call(bf16[128,1024]{1,0:T(8,128)(2,1)} %q_hbm.1, bf16[128,1024]{1,0:T(8,128)(2,1)} %k_hbm.1, bf16[128,1024]{1,0:T(8,128)(2,1)} %v_hbm.1, f32[3,3,1024]{2,1,0:T(4,128)} %fir_hbm.1, f32[1,1024]{1,0:T(1,128)} %bitcast.3, bf16[8,512]{1,0:T(8,128)(2,1)} %taps_hbm.1, s32[1,128]{1,0:T(1,128)} %bitcast.5, ...), custom_call_target="tpu_custom_call" | custom-call | flops 100663296 | bytes 1048576 | tf_op jit(solution)/shard_map/mixer/pallas_call | solution.py:305
  18.0 0.7 %copy.10 = bf16[128,1024]{1,0:T(8,128)(2,1)} copy(bf16[128,1024]{1,0:T(8,128)(2,1)S(1)} %mixer.1) | data formatting | bytes 524288
